TPU v7x, 32 devices: a whole 2x2x4 slice. The times are simulated.
32 devices in a mesh: sub: 8 (over z, y), slab: 4 (over x, core).
Axes of the slice: x: 2, y: 2, z: 4, core: 2. Of those that a mesh axis runs over, the one named last changes fastest.
Arguments:
- mode_shapes: bfloat16 [8, 256, 64], P('sub', 'slab'), may hold values from -0.375 to 0.375
- coupling_k: bfloat16 [8, 256, 1024], P('sub', 'slab'), may hold values from -1 to 1
- coupling_m: bfloat16 [8, 256, 1024], P('sub', 'slab'), may hold values from -1 to 1
- tile_range: int32 [8, 2, 8], P('sub'), may hold values from 0 to 256, as said below
- eigenvalues: float32 [8, 64], P('sub'), may hold values from 0.5 to 8
- adjacency: int32 [8, 8], replicated, may hold values from 0 to 15, as said below
- piece_slot: int32 [16], replicated, may hold values from 0 to 15, as said below
- interface_k: float32 [16, 128, 128], P('sub', 'slab'), may hold values from -0.3 to 0.3
- interface_m: float32 [16, 128, 128], P('sub', 'slab'), may hold values from -0.3 to 0.3
Outputs:
- reduced_k: float32 [16, 128, 128], P('sub', 'slab')
- reduced_m: float32 [16, 128, 128], P('sub', 'slab')
Inputs may be any that keep to these rules, and one draw needn't show every extreme that they name: `adjacency`: each piece's owner device is piece_slot[p] // 2. The 8 pieces of one row have 8 different owner devices, and one owner device is adjacent to every substructure. `piece_slot`: each output row holds exactly one piece. tile_range[i, 0, a] < tile_range[i, 1, a].
All inputs are finite; a program needn't handle non-finite values.
Results may differ from a plain program's by a relative error of at most 0.0034.
Values may be sent and summed in bfloat16 or wider, within the bound.
A program may use at most 64 MiB of HBM per device.

v0:
```python
import jax
import jax.numpy as jnp
from jax import lax
from jax.sharding import PartitionSpec as P


def body(
    mode_shapes,
    coupling_k,
    coupling_m,
    tile_range,
    eigenvalues,
    adjacency,
    piece_slot,
    interface_k,
    interface_m,
):
    row_count = mode_shapes.shape[1]
    mode_count = mode_shapes.shape[2]
    adj_count = adjacency.shape[1]
    piece_width = interface_k.shape[2]
    owned_count = interface_k.shape[0]
    quarter_rows = interface_k.shape[1]
    sub_count = lax.axis_size("sub")
    slab_pos = lax.axis_index("slab")
    sub_pos = lax.axis_index("sub")
    row_index = slab_pos * row_count + lax.iota(jnp.int32, row_count)
    live = (
        (row_index[:, None] >= tile_range[0, 0][None, :])
        & (row_index[:, None] < tile_range[0, 1][None, :])
    ).astype(jnp.bfloat16)
    stiff_rows = (
        coupling_k[0].reshape(row_count, adj_count, piece_width) * live[:, :, None]
    ).reshape(row_count, adj_count * piece_width)
    mass_rows = (
        coupling_m[0].reshape(row_count, adj_count, piece_width) * live[:, :, None]
    ).reshape(row_count, adj_count * piece_width)
    part_s = jnp.einsum("rm,rc->mc", mode_shapes[0], stiff_rows, preferred_element_type=jnp.float32)
    part_v = jnp.einsum("rm,rc->mc", mode_shapes[0], mass_rows, preferred_element_type=jnp.float32)
    proj_s, proj_v = lax.psum((part_s, part_v), "slab")
    eig_held = eigenvalues[0]
    eig_col = eig_held[:, None]
    first = (proj_s * lax.rsqrt(eig_col)).astype(jnp.bfloat16)
    second = (proj_s / eig_col - proj_v).astype(jnp.bfloat16)
    third = proj_v.astype(jnp.bfloat16)
    stacked = jnp.stack([first, second, third]).reshape(3, mode_count, adj_count, piece_width)
    my_slots = piece_slot[adjacency[sub_pos]]
    owner_hot = (
        my_slots[None, :] // owned_count == lax.iota(jnp.int32, sub_count)[:, None]
    ).astype(jnp.bfloat16)
    outgoing = jnp.einsum(
        "oa,kmab->okmb", owner_hot, stacked, preferred_element_type=jnp.float32
    ).astype(jnp.bfloat16)
    incoming = lax.all_to_all(outgoing, "sub", split_axis=0, concat_axis=0, tiled=True)
    all_slots = piece_slot[adjacency]
    targets = sub_pos * owned_count + lax.iota(jnp.int32, owned_count)
    select = jnp.any(all_slots[:, :, None] == targets[None, None, :], axis=1).astype(jnp.bfloat16)

    def piece_gram(weights):
        picked = incoming * weights[:, None, None, None]
        left_side = lax.dynamic_slice_in_dim(picked, slab_pos * quarter_rows, quarter_rows, 3)
        gram_stiff = jnp.einsum(
            "smb,smc->bc", left_side[:, 0], incoming[:, 0], preferred_element_type=jnp.float32
        )
        gram_mass = jnp.einsum(
            "smb,smc->bc", left_side[:, 1], incoming[:, 1], preferred_element_type=jnp.float32
        )
        gram_mass = gram_mass - jnp.einsum(
            "smb,smc->bc", left_side[:, 2], incoming[:, 2], preferred_element_type=jnp.float32
        )
        return (gram_stiff, gram_mass)

    gram_k, gram_m = lax.map(piece_gram, select.T)
    return (interface_k + gram_k, interface_m + gram_m)


def solution(mesh):
    placed = (
        P("sub", "slab", None),
        P("sub", "slab", None),
        P("sub", "slab", None),
        P("sub", None, None),
        P("sub", None),
        P(),
        P(),
        P("sub", "slab", None),
        P("sub", "slab", None),
    )
    return jax.shard_map(
        body,
        mesh=mesh,
        in_specs=placed,
        out_specs=(P("sub", "slab", None), P("sub", "slab", None)),
        check_vma=False,
    )
```

profile of v0, /device:TPU:0, one launch (start us, length us, event | category | flops | bytes accessed | tf_op | source)
XLA Modules:
  0.0 75.6 jit_solution(1284098900973201748)
XLA Ops:
  7.2 0.0 copy-start
  7.2 0.0 all-reduce.3.cloned.1.call-start
  7.2 0.0 copy-start.7
  7.3 0.7 copy-done.7
  7.9 0.1 and_convert_fusion
  8.0 0.1 copy.27
  8.1 0.1 mul.61
  8.2 0.0 copy-start.2
  8.2 0.1 mul.62
  8.3 0.0 copy-done
  8.3 0.8 %copy-done.2 = bf16[1,64,1024]{2,1,0:T(8,128)(2,1)S(1)} copy-done((bf16[1,64,1024]{2,1,0:T(8,128)(2,1)S(1)}, bf16[1,64,1024]{2,1,0:T(8,128)(2,1)}, u32[]{:S(2)}) %copy-start.2) | copy-done | bytes 131096
  9.1 0.0 copy-start.3
  9.1 0.9 %convolution_bitcast_fusion.3 = f32[64,1024]{1,0:T(8,128)} fusion(bf16[1,64,1024]{2,1,0:T(8,128)(2,1)S(1)} %copy-done.2, bf16[1,64,1024]{2,1,0:T(8,128)(2,1)S(1)} %mul.62, bf16[1,64,64]{2,1,0:T(8,128)(2,1)S(1)} %copy-done), kind=kOutput, calls=%fused_computation.19 | convolution fusion | flops 8454144 | bytes 532480 | tf_op jit(solution)/shard_map/rm,rc->mc/dot_general | solution.py:39
  10.1 0.0 copy-done.3
  10.1 0.9 %convolution_bitcast_fusion.4 = f32[64,1024]{1,0:T(8,128)} fusion(bf16[1,64,1024]{2,1,0:T(8,128)(2,1)S(1)} %copy-done.3, bf16[1,64,1024]{2,1,0:T(8,128)(2,1)S(1)} %mul.62, bf16[1,64,64]{2,1,0:T(8,128)(2,1)S(1)} %copy-done), kind=kOutput, calls=%fused_computation.20 | convolution fusion | flops 8454144 | bytes 532480 | tf_op jit(solution)/shard_map/rm,rc->mc/dot_general | solution.py:38
  11.0 0.0 copy-start.8
  11.0 0.0 all-reduce.3.cloned.1.call-update
  11.0 0.6 copy-done.8
  11.7 0.0 copy-start.6
  11.7 0.7 copy-done.6
  12.4 0.0 copy-start.1
  12.4 0.6 copy-done.1
  13.1 0.6 gather_fusion.1
  13.7 33.4 %all-reduce.3.cloned.1.call-done = (f32[64,1024]{1,0:T(8,128)}, f32[64,1024]{1,0:T(8,128)}) async-done(((f32[64,1024]{1,0:T(8,128)}, f32[64,1024]{1,0:T(8,128)}), (f32[64,1024]{1,0:T(8,128)}, f32[64,1024]{1,0:T(8,128)})) %all-reduce.3.cloned.1.call-update) | async-done | bytes 524304 | tf_op jit(solution)/shard_map/psum | solution.py:40
  47.1 1.2 %fusion.10 = (bf16[8,8,8,128]{3,1,2,0:T(8,128)(2,1)S(1)}, bf16[8,8,8,128]{3,1,2,0:T(8,128)(2,1)S(1)}, bf16[8,8,8,128]{3,1,2,0:T(8,128)(2,1)S(1)}) fusion(f32[64,1024]{1,0:T(8,128)} %get-tuple-element.117, f32[64]{0:T(128)S(1)} %bitcast_rsqrt_fusion, f32[64,1024]{1,0:T(8,128)} %get-tuple-element.116, f32[64]{0:T(128)S(1)} %bitcast.108), kind=kLoop, calls=%fused_computation.28 | loop fusion | flops 393216 | bytes 918016
  48.4 0.2 convolution_convert_fusion
  48.7 0.8 %copy.28 = bf16[8,3,64,128]{3,2,1,0:T(8,128)(2,1)} copy(bf16[8,3,64,128]{3,0,2,1:T(8,128)(2,1)S(1)} %convolution_convert_fusion) | data formatting | bytes 786432 | tf_op jit(solution)/shard_map/convert_element_type | solution.py:53
  49.5 5.5 %all-to-all-start = ((bf16[8,3,64,128]{3,2,1,0:T(8,128)(2,1)}), bf16[8,3,64,128]{3,2,1,0:T(8,128)(2,1)S(1)}, u32[]{:S(2)}, u32[]{:S(2)}) async-start(bf16[8,3,64,128]{3,2,1,0:T(8,128)(2,1)} %copy.28), calls=%async_computation | async-start | bytes 786432 | tf_op jit(solution)/shard_map/all_to_all | solution.py:54
  55.0 0.1 reshape.165
  55.1 0.8 %gather_fusion = s32[64]{0:T(128)S(1)} fusion(s32[16]{0:T(128)S(1)} %copy-done.1, s32[1024]{0:T(1024)S(1)} %pad_clamp_fusion.1), kind=kCustom, calls=%fused_computation | custom fusion | bytes 768 | tf_op jit(solution)/shard_map/gather | solution.py:55
  55.9 0.1 reshape.164
  56.0 0.2 compare_reduce_fusion
  56.2 9.6 %all-to-all-done = bf16[8,3,64,128]{3,2,1,0:T(8,128)(2,1)S(1)} async-done(((bf16[8,3,64,128]{3,2,1,0:T(8,128)(2,1)}), bf16[8,3,64,128]{3,2,1,0:T(8,128)(2,1)S(1)}, u32[]{:S(2)}, u32[]{:S(2)}) %all-to-all-start) | async-done | bytes 393248 | tf_op jit(solution)/shard_map/all_to_all | solution.py:54
  65.8 0.0 copy-start.4
  65.8 1.6 %while.14 = (s32[]{:T(128)}, f32[2,32,128]{2,1,0:T(8,128)S(1)}, f32[2,32,128]{2,1,0:T(8,128)S(1)}, bf16[2,8]{1,0:T(2,128)(2,1)S(1)}, bf16[8,3,64,128]{3,2,1,0:T(8,128)(2,1)S(1)}, /*index=5*/s32[]{:T(128)}, s32[]{:T(128)}) while((s32[]{:T(128)}, f32[2,32,128]{2,1,0:T(8,128)S(1)}, f32[2,32,128]{2,1,0:T(8,128)S(1)}, bf16[2,8]{1,0:T(2,128)(2,1)S(1)}, ...), condition=%wide.region_4.5_spmd, body=%wide.region_3.4_spmd.sunk | while | flops 12783618 | bytes 1048717 | solution.py:73
  65.8 0.2 dynamic-slice_multiply_fusion.2
  66.0 0.2 convolution_bitcast_fusion.6
  66.2 0.2 fusion.37
  66.4 0.2 fusion.36
  66.6 0.2 dynamic-slice_multiply_fusion.2
  66.8 0.2 convolution_bitcast_fusion.6
  67.0 0.2 fusion.37
  67.2 0.2 fusion.36
  67.4 0.0 copy-done.4
  67.4 0.0 copy-start.5
  67.4 0.6 add.74
  68.0 0.1 copy-done.5
  68.1 0.6 add.75
  (17 shorter events, 0.1 us)
Async XLA Ops:
  7.2 1.2 %copy-start = (bf16[1,64,64]{2,1,0:T(8,128)(2,1)S(1)}, bf16[1,64,64]{2,1,0:T(8,128)(2,1)}, u32[]{:S(2)}) copy-start(bf16[1,64,64]{2,1,0:T(8,128)(2,1)} %param.11) | copy-start | bytes 24580
  7.2 39.9 %all-reduce.3.cloned.1.call-start = ((), (), s32[]{:S(2)}) async-start(), calls=%async_computation.1 | async-start | bytes 1048576 | tf_op jit(solution)/shard_map/psum | solution.py:40
  7.2 0.7 copy-start.7
  8.2 0.9 %copy-start.2 = (bf16[1,64,1024]{2,1,0:T(8,128)(2,1)S(1)}, bf16[1,64,1024]{2,1,0:T(8,128)(2,1)}, u32[]{:S(2)}) copy-start(bf16[1,64,1024]{2,1,0:T(8,128)(2,1)} %param.13) | copy-start | bytes 393220
  9.1 0.9 %copy-start.3 = (bf16[1,64,1024]{2,1,0:T(8,128)(2,1)S(1)}, bf16[1,64,1024]{2,1,0:T(8,128)(2,1)}, u32[]{:S(2)}) copy-start(bf16[1,64,1024]{2,1,0:T(8,128)(2,1)} %param.12) | copy-start | bytes 393220
  11.0 0.7 copy-start.8
  11.7 0.7 copy-start.6
  12.4 0.7 copy-start.1
  49.5 16.3 %all-to-all-start = ((bf16[8,3,64,128]{3,2,1,0:T(8,128)(2,1)}), bf16[8,3,64,128]{3,2,1,0:T(8,128)(2,1)S(1)}, u32[]{:S(2)}, u32[]{:S(2)}) async-start(bf16[8,3,64,128]{3,2,1,0:T(8,128)(2,1)} %copy.28), calls=%async_computation | async-start | bytes 786432 | tf_op jit(solution)/shard_map/all_to_all | solution.py:54
  65.8 1.6 %copy-start.4 = (f32[2,32,128]{2,1,0:T(8,128)S(1)}, f32[2,32,128]{2,1,0:T(8,128)}, u32[]{:S(2)}) copy-start(f32[2,32,128]{2,1,0:T(8,128)} %param.18) | copy-start | bytes 98308
  67.4 0.8 %copy-start.5 = (f32[2,32,128]{2,1,0:T(8,128)S(1)}, f32[2,32,128]{2,1,0:T(8,128)}, u32[]{:S(2)}) copy-start(f32[2,32,128]{2,1,0:T(8,128)} %param.19) | copy-start | bytes 98308
Sparse Core Ops, SparseCore 0:
  11.2 35.8 all-reduce.2
where the time goes:
time: 76 us; the launch traced here: 75.6 us
  waiting for transfers between devices  43 us (57%)
  between operations  14.2 us (19%)
  local copies, waits for them, and re-layouts  6.4 us (8%)
  starting transfers between devices  5.55 us (7%)
  matrix products  3.24 us (4%)
  other arithmetic  3.21 us (4%)
    psum x1, waiting for transfers between devices, body(): proj_s, proj_v = lax.psum((part_s, part_v), 'slab')  33.4 us
    all_to_all x1, waiting for transfers between devices, body(): lax.all_to_all(outgoing, 'sub', split_axis=0, concat_axis=0, tiled=True)  9.58 us
    all_to_all x1, starting transfers between devices, body(): lax.all_to_all(outgoing, 'sub', split_axis=0, concat_axis=0, tiled=True)  5.52 us
    unnamed x21, local copies, waits for them, and re-layouts  3.67 us
  transfers between devices with their start and end apart: 2, of which 2 were waited for; matrix products, arithmetic and copies ran while one was open for 2% of the time, Pallas kernels for 0%

commit v1 on v0

--- a/solution.py
+++ b/solution.py
@@ -1,10 +1,290 @@
+import functools
+
 import jax
 import jax.numpy as jnp
 from jax import lax
+from jax.experimental import pallas as pl
+from jax.experimental.pallas import tpu as pltpu
 from jax.sharding import PartitionSpec as P
 
-
-def body(
+MESH = pl.DeviceIdType.MESH
+
+
+def contract_rows(left, right):
+    return lax.dot_general(
+        left, right, (((0,), (0,)), ((), ())), preferred_element_type=jnp.float32
+    )
+
+
+def kernel(
+    subs,
+    slabs,
+    adjacency,
+    piece_slot,
+    tile_range,
+    eigenvalues,
+    modes,
+    coupling_k,
+    coupling_m,
+    interface_k,
+    interface_m,
+    reduced_k,
+    reduced_m,
+    tile_k,
+    tile_m,
+    outgoing,
+    columns,
+    all_modes,
+    blocks,
+    arrived,
+    local_sem,
+    modes_send,
+    modes_recv,
+    columns_send,
+    columns_recv,
+    blocks_send,
+    blocks_recv,
+):
+    sub = lax.axis_index("sub")
+    slab = lax.axis_index("slab")
+    group = subs // slabs
+    adj = adjacency.shape[1]
+    owned, quarter, width = interface_k.shape
+    rows = modes.shape[1]
+    home = sub // group
+
+    loads = [
+        pltpu.make_async_copy(
+            whole.at[0, :, a * width : (a + 1) * width], tile.at[a], local_sem.at[kind, a]
+        )
+        for a in range(adj)
+        for kind, (whole, tile) in enumerate(((coupling_k, tile_k), (coupling_m, tile_m)))
+    ]
+    loads.append(pltpu.make_async_copy(modes.at[0], all_modes.at[slab], modes_recv.at[slab]))
+    for load in loads:
+        load.start()
+
+    barrier = pltpu.get_barrier_semaphore()
+    for turn in range(1, slabs):
+        pl.semaphore_signal(
+            barrier, inc=1, device_id=(sub, lax.rem(slab + turn, slabs)), device_id_type=MESH
+        )
+    for turn in range(1, subs):
+        pl.semaphore_signal(
+            barrier, inc=1, device_id=(lax.rem(sub + turn, subs), home), device_id_type=MESH
+        )
+
+    @pl.when(home != slab)
+    def _():
+        pl.semaphore_signal(barrier, inc=1, device_id=(sub, home), device_id_type=MESH)
+
+    slots = [piece_slot[adjacency[sub, a]] for a in range(adj)]
+
+    def owner_of(part, step):
+        return part * group + lax.rem(step + sub + 1, group)
+
+    for load in loads[:-1]:
+        load.wait()
+    row_index = slab * rows + lax.broadcasted_iota(jnp.int32, (rows, width), 0)
+    for turn in list(range(1, slabs)) + [0]:
+        part = lax.rem(slab + turn, slabs)
+        for step in range(group):
+            owner = owner_of(part, step)
+            place = jnp.int32(0)
+            for a in range(adj):
+                mine = (slots[a] >= owner * owned) & (slots[a] < (owner + 1) * owned)
+                place = jnp.where(mine, jnp.int32(a), place)
+            start = tile_range[0, 0, place]
+            finish = tile_range[0, 1, place]
+            live = ((row_index >= start) & (row_index < finish)).astype(jnp.float32)
+            live = live.astype(jnp.bfloat16)
+            stiff = tile_k[place] * live
+            mass = tile_m[place] * live
+            if turn == 0:
+                columns[step, slab, :, 0:width] = stiff
+                columns[step, slab, :, width:] = mass
+            else:
+                outgoing[step, turn - 1, :, 0:width] = stiff
+                outgoing[step, turn - 1, :, width:] = mass
+
+    @pl.when(home != slab)
+    def _():
+        pl.semaphore_wait(barrier, slabs - 1 + group * slabs)
+
+    @pl.when(home == slab)
+    def _():
+        pl.semaphore_wait(barrier, slabs - 1 + group * slabs - 1)
+
+    sends = []
+    for turn in range(1, slabs):
+        part = lax.rem(slab + turn, slabs)
+        copy = pltpu.make_async_remote_copy(
+            src_ref=modes.at[0],
+            dst_ref=all_modes.at[slab],
+            send_sem=modes_send.at[turn - 1],
+            recv_sem=modes_recv.at[slab],
+            device_id=(sub, part),
+            device_id_type=MESH,
+        )
+        copy.start()
+        sends.append(copy)
+    for step in range(group):
+        for turn in range(1, slabs):
+            part = lax.rem(slab + turn, slabs)
+            copy = pltpu.make_async_remote_copy(
+                src_ref=outgoing.at[step, turn - 1],
+                dst_ref=columns.at[step, slab],
+                send_sem=columns_send.at[step, turn - 1],
+                recv_sem=columns_recv.at[step, slab],
+                device_id=(sub, part),
+                device_id_type=MESH,
+            )
+            copy.start()
+            sends.append(copy)
+
+    takes = []
+    for other in range(subs):
+        theirs = [piece_slot[adjacency[other, a]] for a in range(adj)]
+        takes.append([
+            functools.reduce(
+                lambda x, y: x | y,
+                [(slot == sub * owned + q).astype(jnp.int32) for slot in theirs],
+            )
+            for q in range(owned)
+        ])
+    eig = jnp.broadcast_to(eigenvalues[...], (width, modes.shape[2])).T
+    root = lax.rsqrt(eig)
+
+    loads[-1].wait()
+    for turn in range(1, slabs):
+        part = lax.rem(slab + turn, slabs)
+        pltpu.make_async_copy(all_modes.at[part], all_modes.at[part], modes_recv.at[part]).wait()
+    basis = all_modes[...].reshape(slabs * rows, modes.shape[2])
+    for step in range(group):
+        for turn in range(1, slabs):
+            part = lax.rem(slab + turn, slabs)
+            pltpu.make_async_copy(
+                columns.at[step, part], columns.at[step, part], columns_recv.at[step, part]
+            ).wait()
+        proj = contract_rows(basis, columns[step].reshape(slabs * rows, 2 * width))
+        proj_s, proj_v = proj[:, :width], proj[:, width:]
+        first = (proj_s * root).astype(jnp.bfloat16)
+        second = (proj_s / eig - proj_v).astype(jnp.bfloat16)
+        third = proj_v.astype(jnp.bfloat16)
+        gram_k = contract_rows(first, first)
+        gram_m = contract_rows(
+            jnp.concatenate([second, third]), jnp.concatenate([second, -third])
+        )
+        blocks[step, :, 0] = gram_k.astype(jnp.bfloat16).reshape(slabs, quarter, width)
+        blocks[step, :, 1] = gram_m.astype(jnp.bfloat16).reshape(slabs, quarter, width)
+        owner = owner_of(slab, step)
+        for turn in range(1, slabs + 1):
+            part = lax.rem(slab + turn, slabs)
+            copy = pltpu.make_async_remote_copy(
+                src_ref=blocks.at[step, part],
+                dst_ref=arrived.at[sub],
+                send_sem=blocks_send.at[step, turn - 1],
+                recv_sem=blocks_recv.at[sub],
+                device_id=(owner, part),
+                device_id_type=MESH,
+            )
+            if turn < slabs:
+                copy.start()
+                sends.append(copy)
+            else:
+                pl.when(owner != sub)(copy.start)
+
+                @pl.when(owner == sub)
+                def _():
+                    arrived[sub] = blocks[step, slab]
+
+    total = [[interface_k[q] for q in range(owned)], [interface_m[q] for q in range(owned)]]
+    for other in range(subs):
+
+        @pl.when((other != sub) | (home != slab))
+        def _():
+            pltpu.make_async_copy(
+                arrived.at[other], arrived.at[other], blocks_recv.at[other]
+            ).wait()
+
+        for kind in range(2):
+            term = arrived[other, kind].astype(jnp.float32)
+            for q in range(owned):
+                total[kind][q] = total[kind][q] + jnp.where(takes[other][q] > 0, term, 0.0)
+    for q in range(owned):
+        reduced_k[q] = total[0][q]
+        reduced_m[q] = total[1][q]
+
+    for copy in sends:
+        copy.wait_send()
+    for step in range(group):
+
+        @pl.when(owner_of(slab, step) != sub)
+        def _():
+            pltpu.make_async_copy(
+                blocks.at[step, slab], blocks.at[step, slab], blocks_send.at[step, slabs - 1]
+            ).wait()
+
+
+def dense_body(
+    subs,
+    slabs,
+    mode_shapes,
+    coupling_k,
+    coupling_m,
+    tile_range,
+    eigenvalues,
+    adjacency,
+    piece_slot,
+    interface_k,
+    interface_m,
+):
+    _, rows, mode_count = mode_shapes.shape
+    adj = adjacency.shape[1]
+    owned, quarter, width = interface_k.shape
+    group = subs // slabs
+    vmem = pl.BlockSpec(memory_space=pltpu.VMEM)
+    smem = pl.BlockSpec(memory_space=pltpu.SMEM)
+    hbm = pl.BlockSpec(memory_space=pl.ANY)
+    out = jax.ShapeDtypeStruct(interface_k.shape, interface_k.dtype)
+    return pl.pallas_call(
+        functools.partial(kernel, subs, slabs),
+        out_shape=(out, out),
+        in_specs=[smem, smem, smem, vmem, hbm, hbm, hbm, vmem, vmem],
+        out_specs=(vmem, vmem),
+        scratch_shapes=[
+            pltpu.VMEM((adj, rows, width), jnp.bfloat16),
+            pltpu.VMEM((adj, rows, width), jnp.bfloat16),
+            pltpu.VMEM((group, slabs - 1, rows, 2 * width), jnp.bfloat16),
+            pltpu.VMEM((group, slabs, rows, 2 * width), jnp.bfloat16),
+            pltpu.VMEM((slabs, rows, mode_count), jnp.bfloat16),
+            pltpu.VMEM((group, slabs, 2, quarter, width), jnp.bfloat16),
+            pltpu.VMEM((subs, 2, quarter, width), jnp.bfloat16),
+            pltpu.SemaphoreType.DMA((2, adj)),
+            pltpu.SemaphoreType.DMA((slabs - 1,)),
+            pltpu.SemaphoreType.DMA((slabs,)),
+            pltpu.SemaphoreType.DMA((group, slabs - 1)),
+            pltpu.SemaphoreType.DMA((group, slabs)),
+            pltpu.SemaphoreType.DMA((group, slabs)),
+            pltpu.SemaphoreType.DMA((subs,)),
+        ],
+        compiler_params=pltpu.CompilerParams(
+            collective_id=0, has_side_effects=True, vmem_limit_bytes=16 * 1024 * 1024
+        ),
+    )(
+        adjacency,
+        piece_slot,
+        tile_range,
+        eigenvalues,
+        mode_shapes,
+        coupling_k,
+        coupling_m,
+        interface_k,
+        interface_m,
+    )
+
+
+def sparse_body(
     mode_shapes,
     coupling_k,
     coupling_m,
@@ -74,6 +354,13 @@
     return (interface_k + gram_k, interface_m + gram_m)
 
 
+def body(subs, slabs, *arrays):
+    adjacency = arrays[5]
+    if adjacency.shape[1] == subs and subs % slabs == 0:
+        return dense_body(subs, slabs, *arrays)
+    return sparse_body(*arrays)
+
+
 def solution(mesh):
     placed = (
         P("sub", "slab", None),
@@ -87,7 +374,7 @@
         P("sub", "slab", None),
     )
     return jax.shard_map(
-        body,
+        functools.partial(body, mesh.shape["sub"], mesh.shape["slab"]),
         mesh=mesh,
         in_specs=placed,
         out_specs=(P("sub", "slab", None), P("sub", "slab", None)),

time: 76 us -> 28.1 us (0.37)
  waiting for transfers between devices: 43 us -> 0 us
  Pallas kernels: 0 us -> 19.1 us
  between operations: 14.2 us -> 0.66 us
  starting transfers between devices: 5.55 us -> 0 us
  matrix products: 3.24 us -> 0 us
  other arithmetic: 3.21 us -> 0 us
  local copies, waits for them, and re-layouts: 6.4 us -> 7.94 us
    psum x1 -> x0, waiting for transfers between devices: 33.4 us -> none  [body(): proj_s, proj_v = lax.psum((part_s, part_v), 'slab')]
    pallas_call x0 -> x1, Pallas kernels: none -> 19.1 us  [dense_body(): pl.pallas_call(functools.partial(kernel, subs, slabs), out_shape=(out, ou...]
    all_to_all x1 -> x0, waiting for transfers between devices: 9.58 us -> none  [body(): lax.all_to_all(outgoing, 'sub', split_axis=0, concat_axis=0, tiled=True)]
    all_to_all x1 -> x0, starting transfers between devices: 5.52 us -> none  [body(): lax.all_to_all(outgoing, 'sub', split_axis=0, concat_axis=0, tiled=True)]
    unnamed x21 -> x20, local copies, waits for them, and re-layouts: 3.67 us -> 7.94 us
    dot_general x9 -> x0, matrix products: 3.24 us -> none  [the longest x1 0.94 us: body(): jnp.einsum('rm,rc->mc', mode_shapes[0], stiff_rows, preferred_element_typ...]
    gather x3 -> x0, local copies, waits for them, and re-layouts: 1.5 us -> none  [the longest x2 0.85 us: body(): all_slots = piece_slot[adjacency]]
    add x4 -> x0, other arithmetic: 1.25 us -> none  [the longest x2 1.24 us: body(): return (interface_k + gram_k, interface_m + gram_m)]
  transfers between devices with their start and end apart: 2 -> 0, of which waited for: 2 -> 0; matrix products, arithmetic and copies ran while one was open for 2% -> 0% of each run, Pallas kernels for 0% -> 0%
where the time goes in v1:
time: 28.1 us; the launch traced here: 27.7 us
  Pallas kernels  19.1 us (68%)
  local copies, waits for them, and re-layouts  7.94 us (28%)
  between operations  0.66 us (2%)
    pallas_call x1, Pallas kernels, dense_body(): pl.pallas_call(functools.partial(kernel, subs, slabs), out_shape=(out, ou...  19.1 us
    unnamed x20, local copies, waits for them, and re-layouts  7.94 us

profile of v1, /device:TPU:0, one launch (start us, length us, event | category | flops | bytes accessed | tf_op | source)
XLA Modules:
  0.0 27.7 jit_solution(2488565920050583914)
XLA Ops:
  0.6 0.0 copy-start
  0.6 0.9 %copy-done = bf16[1,64,1024]{2,1,0:T(8,128)(2,1)S(1)} copy-done((bf16[1,64,1024]{2,1,0:T(8,128)(2,1)S(1)}, bf16[1,64,1024]{2,1,0:T(8,128)(2,1)}, u32[]{:S(2)}) %copy-start) | copy-done | bytes 131096
  1.5 0.0 copy-start.1
  1.5 0.9 %copy-done.1 = bf16[1,64,1024]{2,1,0:T(8,128)(2,1)S(1)} copy-done((bf16[1,64,1024]{2,1,0:T(8,128)(2,1)S(1)}, bf16[1,64,1024]{2,1,0:T(8,128)(2,1)}, u32[]{:S(2)}) %copy-start.1) | copy-done | bytes 131096
  2.4 0.0 copy-start.2
  2.4 0.8 %copy-done.2 = f32[2,32,128]{2,1,0:T(8,128)S(1)} copy-done((f32[2,32,128]{2,1,0:T(8,128)S(1)}, f32[2,32,128]{2,1,0:T(8,128)}, u32[]{:S(2)}) %copy-start.2) | copy-done | bytes 32792
  3.2 0.0 copy-start.3
  3.2 0.8 %copy-done.3 = f32[2,32,128]{2,1,0:T(8,128)S(1)} copy-done((f32[2,32,128]{2,1,0:T(8,128)S(1)}, f32[2,32,128]{2,1,0:T(8,128)}, u32[]{:S(2)}) %copy-start.3) | copy-done | bytes 32792
  4.0 0.0 copy-start.4
  4.0 0.7 %copy-done.4 = bf16[1,64,64]{2,1,0:T(8,128)(2,1)S(1)} copy-done((bf16[1,64,64]{2,1,0:T(8,128)(2,1)S(1)}, bf16[1,64,64]{2,1,0:T(8,128)(2,1)}, u32[]{:S(2)}) %copy-start.4) | copy-done | bytes 8216
  4.7 0.0 copy-start.5
  4.7 0.7 %copy-done.5 = s32[8,8]{1,0:T(8,128)S(1)} copy-done((s32[8,8]{1,0:T(8,128)S(1)}, s32[8,8]{1,0:T(8,128)}, u32[]{:S(2)}) %copy-start.5) | copy-done | bytes 280
  5.4 0.0 copy-start.6
  5.4 0.7 %copy-done.6 = s32[1,2,8]{2,1,0:T(2,128)S(1)} copy-done((s32[1,2,8]{2,1,0:T(2,128)S(1)}, s32[1,2,8]{2,1,0:T(2,128)}, u32[]{:S(2)}) %copy-start.6) | copy-done | bytes 88
  6.0 0.0 copy-start.7
  6.0 0.7 %copy-done.7 = s32[16]{0:T(128)S(1)} copy-done((s32[16]{0:T(128)S(1)}, s32[16]{0:T(128)}, u32[]{:S(2)}) %copy-start.7) | copy-done | bytes 88
  6.7 0.0 copy-start.8
  6.7 0.7 %copy-done.8 = f32[1,64]{1,0:T(1,128)S(1)} copy-done((f32[1,64]{1,0:T(1,128)S(1)}, f32[1,64]{1,0:T(1,128)}, u32[]{:S(2)}) %copy-start.8) | copy-done | bytes 280
  7.4 19.1 %shard_map.104 = (f32[2,32,128]{2,1,0:T(8,128)S(1)}, f32[2,32,128]{2,1,0:T(8,128)S(1)}) custom-call(s32[8,8]{1,0:T(8,128)S(1)} %copy-done.5, s32[16]{0:T(128)S(1)} %copy-done.7, s32[1,2,8]{2,1,0:T(2,128)S(1)} %copy-done.6, f32[1,64]{1,0:T(1,128)S(1)} %copy-done.8, bf16[1,64,64]{2,1,0:T(8,128)(2,1)S(1)} %copy-done.4, bf16[1,64,1024]{2,1,0:T(8,128)(2,1)S(1)} %copy-done, ...), custom_call_target="tpu_custom_call" | custom-call | tf_op jit(solution)/shard_map/pallas_call | solution.py:250
  26.4 0.6 %copy.13 = f32[2,32,128]{2,1,0:T(8,128)} copy(f32[2,32,128]{2,1,0:T(8,128)S(1)} %get-tuple-element.4) | data formatting | bytes 65536
  27.0 0.6 %copy.14 = f32[2,32,128]{2,1,0:T(8,128)} copy(f32[2,32,128]{2,1,0:T(8,128)S(1)} %get-tuple-element.5) | data formatting | bytes 65536
Async XLA Ops:
  0.6 0.9 %copy-start = (bf16[1,64,1024]{2,1,0:T(8,128)(2,1)S(1)}, bf16[1,64,1024]{2,1,0:T(8,128)(2,1)}, u32[]{:S(2)}) copy-start(bf16[1,64,1024]{2,1,0:T(8,128)(2,1)} %coupling_k.1) | copy-start | bytes 393220
  1.5 0.9 %copy-start.1 = (bf16[1,64,1024]{2,1,0:T(8,128)(2,1)S(1)}, bf16[1,64,1024]{2,1,0:T(8,128)(2,1)}, u32[]{:S(2)}) copy-start(bf16[1,64,1024]{2,1,0:T(8,128)(2,1)} %coupling_m.1) | copy-start | bytes 393220
  2.4 0.8 %copy-start.2 = (f32[2,32,128]{2,1,0:T(8,128)S(1)}, f32[2,32,128]{2,1,0:T(8,128)}, u32[]{:S(2)}) copy-start(f32[2,32,128]{2,1,0:T(8,128)} %interface_k.1) | copy-start | bytes 98308
  3.2 0.8 %copy-start.3 = (f32[2,32,128]{2,1,0:T(8,128)S(1)}, f32[2,32,128]{2,1,0:T(8,128)}, u32[]{:S(2)}) copy-start(f32[2,32,128]{2,1,0:T(8,128)} %interface_m.1) | copy-start | bytes 98308
  4.0 0.7 %copy-start.4 = (bf16[1,64,64]{2,1,0:T(8,128)(2,1)S(1)}, bf16[1,64,64]{2,1,0:T(8,128)(2,1)}, u32[]{:S(2)}) copy-start(bf16[1,64,64]{2,1,0:T(8,128)(2,1)} %modes.1) | copy-start | bytes 24580
  4.7 0.7 %copy-start.5 = (s32[8,8]{1,0:T(8,128)S(1)}, s32[8,8]{1,0:T(8,128)}, u32[]{:S(2)}) copy-start(s32[8,8]{1,0:T(8,128)} %adjacency.1) | copy-start | bytes 772
  5.4 0.7 %copy-start.6 = (s32[1,2,8]{2,1,0:T(2,128)S(1)}, s32[1,2,8]{2,1,0:T(2,128)}, u32[]{:S(2)}) copy-start(s32[1,2,8]{2,1,0:T(2,128)} %tile_range.1) | copy-start | bytes 196
  6.0 0.7 %copy-start.7 = (s32[16]{0:T(128)S(1)}, s32[16]{0:T(128)}, u32[]{:S(2)}) copy-start(s32[16]{0:T(128)} %piece_slot.1) | copy-start | bytes 196
  6.7 0.7 %copy-start.8 = (f32[1,64]{1,0:T(1,128)S(1)}, f32[1,64]{1,0:T(1,128)}, u32[]{:S(2)}) copy-start(f32[1,64]{1,0:T(1,128)} %eigenvalues.1) | copy-start | bytes 772

commit v2 on v1

--- a/solution.py
+++ b/solution.py
@@ -19,17 +19,23 @@
 def kernel(
     subs,
     slabs,
+    adjacency_hbm,
+    piece_slot_hbm,
+    tile_range_hbm,
+    eigenvalues_hbm,
+    modes,
+    coupling_k,
+    coupling_m,
+    interface_k_hbm,
+    interface_m_hbm,
+    reduced_k,
+    reduced_m,
     adjacency,
     piece_slot,
     tile_range,
     eigenvalues,
-    modes,
-    coupling_k,
-    coupling_m,
     interface_k,
     interface_m,
-    reduced_k,
-    reduced_m,
     tile_k,
     tile_m,
     outgoing,
@@ -37,6 +43,7 @@
     all_modes,
     blocks,
     arrived,
+    small_sem,
     local_sem,
     modes_send,
     modes_recv,
@@ -60,6 +67,21 @@
         for a in range(adj)
         for kind, (whole, tile) in enumerate(((coupling_k, tile_k), (coupling_m, tile_m)))
     ]
+    routing = [
+        pltpu.make_async_copy(whole, held, small_sem.at[n])
+        for n, (whole, held) in enumerate((
+            (adjacency_hbm, adjacency), (piece_slot_hbm, piece_slot), (tile_range_hbm, tile_range)
+        ))
+    ]
+    late = [
+        pltpu.make_async_copy(whole, held, small_sem.at[3 + n])
+        for n, (whole, held) in enumerate((
+            (eigenvalues_hbm, eigenvalues),
+            (interface_k_hbm, interface_k),
+            (interface_m_hbm, interface_m),
+        ))
+    ]
+    loads = routing + loads + late
     loads.append(pltpu.make_async_copy(modes.at[0], all_modes.at[slab], modes_recv.at[slab]))
     for load in loads:
         load.start()
@@ -78,12 +100,14 @@
     def _():
         pl.semaphore_signal(barrier, inc=1, device_id=(sub, home), device_id_type=MESH)
 
+    for load in routing:
+        load.wait()
     slots = [piece_slot[adjacency[sub, a]] for a in range(adj)]
 
     def owner_of(part, step):
         return part * group + lax.rem(step + sub + 1, group)
 
-    for load in loads[:-1]:
+    for load in loads[len(routing) : -1 - len(late)]:
         load.wait()
     row_index = slab * rows + lax.broadcasted_iota(jnp.int32, (rows, width), 0)
     for turn in list(range(1, slabs)) + [0]:
@@ -152,6 +176,8 @@
             )
             for q in range(owned)
         ])
+    for load in late:
+        load.wait()
     eig = jnp.broadcast_to(eigenvalues[...], (width, modes.shape[2])).T
     root = lax.rsqrt(eig)
 
@@ -244,15 +270,20 @@
     owned, quarter, width = interface_k.shape
     group = subs // slabs
     vmem = pl.BlockSpec(memory_space=pltpu.VMEM)
-    smem = pl.BlockSpec(memory_space=pltpu.SMEM)
-    hbm = pl.BlockSpec(memory_space=pl.ANY)
+    hbm = pl.BlockSpec(memory_space=pltpu.HBM)
     out = jax.ShapeDtypeStruct(interface_k.shape, interface_k.dtype)
     return pl.pallas_call(
         functools.partial(kernel, subs, slabs),
         out_shape=(out, out),
-        in_specs=[smem, smem, smem, vmem, hbm, hbm, hbm, vmem, vmem],
+        in_specs=[hbm] * 9,
         out_specs=(vmem, vmem),
         scratch_shapes=[
+            pltpu.SMEM(adjacency.shape, adjacency.dtype),
+            pltpu.SMEM(piece_slot.shape, piece_slot.dtype),
+            pltpu.SMEM(tile_range.shape, tile_range.dtype),
+            pltpu.VMEM(eigenvalues.shape, eigenvalues.dtype),
+            pltpu.VMEM(interface_k.shape, interface_k.dtype),
+            pltpu.VMEM(interface_m.shape, interface_m.dtype),
             pltpu.VMEM((adj, rows, width), jnp.bfloat16),
             pltpu.VMEM((adj, rows, width), jnp.bfloat16),
             pltpu.VMEM((group, slabs - 1, rows, 2 * width), jnp.bfloat16),
@@ -260,6 +291,7 @@
             pltpu.VMEM((slabs, rows, mode_count), jnp.bfloat16),
             pltpu.VMEM((group, slabs, 2, quarter, width), jnp.bfloat16),
             pltpu.VMEM((subs, 2, quarter, width), jnp.bfloat16),
+            pltpu.SemaphoreType.DMA((6,)),
             pltpu.SemaphoreType.DMA((2, adj)),
             pltpu.SemaphoreType.DMA((slabs - 1,)),
             pltpu.SemaphoreType.DMA((slabs,)),
@@ -269,7 +301,7 @@
             pltpu.SemaphoreType.DMA((subs,)),
         ],
         compiler_params=pltpu.CompilerParams(
-            collective_id=0, has_side_effects=True, vmem_limit_bytes=16 * 1024 * 1024
+            collective_id=0, has_side_effects=True, vmem_limit_bytes=64 * 1024 * 1024
         ),
     )(
         adjacency,

time: 28.1 us -> 22.2 us (0.79)
  local copies, waits for them, and re-layouts: 7.94 us -> 2 us
    unnamed x20 -> x4, local copies, waits for them, and re-layouts: 7.94 us -> 2 us
where the time goes in v2:
time: 22.2 us; the launch traced here: 21.9 us
  Pallas kernels  19.3 us (87%)
  local copies, waits for them, and re-layouts  2 us (9%)
  between operations  0.65 us (3%)
    pallas_call x1, Pallas kernels, dense_body(): pl.pallas_call(functools.partial(kernel, subs, slabs), out_shape=(out, ou...  19.3 us
    unnamed x4, local copies, waits for them, and re-layouts  2 us

profile of v2, /device:TPU:0, one launch (start us, length us, event | category | flops | bytes accessed | tf_op | source)
XLA Modules:
  0.0 21.9 jit_solution(1965581682581173965)
XLA Ops:
  0.6 19.3 %shard_map.104 = (f32[2,32,128]{2,1,0:T(8,128)}, f32[2,32,128]{2,1,0:T(8,128)}) custom-call(s32[8,8]{1,0:T(8,128)} %adjacency_hbm.1, s32[16]{0:T(128)} %piece_slot_hbm.1, s32[1,2,8]{2,1,0:T(2,128)} %tile_range_hbm.1, f32[1,64]{1,0:T(1,128)} %eigenvalues_hbm.1, bf16[1,64,64]{2,1,0:T(8,128)(2,1)} %modes.1, bf16[1,64,1024]{2,1,0:T(8,128)(2,1)} %coupling_k.1, ...), custom_call_target="tpu_custom_call" | custom-call | tf_op jit(solution)/shard_map/pallas_call | solution.py:275
  19.9 0.0 copy-start
  19.9 1.4 %copy.13 = f32[2,32,128]{2,1,0:T(8,128)} copy(f32[2,32,128]{2,1,0:T(8,128)} %get-tuple-element.4) | data formatting | bytes 65536
  21.3 0.0 copy-done
  21.3 0.6 %copy.14 = f32[2,32,128]{2,1,0:T(8,128)} copy(f32[2,32,128]{2,1,0:T(8,128)S(1)} %copy-done) | data formatting | bytes 65536
Async XLA Ops:
  19.9 1.4 %copy-start = (f32[2,32,128]{2,1,0:T(8,128)S(1)}, f32[2,32,128]{2,1,0:T(8,128)}, u32[]{:S(2)}) copy-start(f32[2,32,128]{2,1,0:T(8,128)} %get-tuple-element.5) | copy-start | bytes 98308

commit v3 on v2

--- a/solution.py
+++ b/solution.py
@@ -26,16 +26,11 @@
     modes,
     coupling_k,
     coupling_m,
-    interface_k_hbm,
-    interface_m_hbm,
-    reduced_k,
-    reduced_m,
+    gram,
     adjacency,
     piece_slot,
     tile_range,
     eigenvalues,
-    interface_k,
-    interface_m,
     tile_k,
     tile_m,
     outgoing,
@@ -56,7 +51,7 @@
     slab = lax.axis_index("slab")
     group = subs // slabs
     adj = adjacency.shape[1]
-    owned, quarter, width = interface_k.shape
+    _, owned, quarter, width = gram.shape
     rows = modes.shape[1]
     home = sub // group
 
@@ -75,11 +70,7 @@
     ]
     late = [
         pltpu.make_async_copy(whole, held, small_sem.at[3 + n])
-        for n, (whole, held) in enumerate((
-            (eigenvalues_hbm, eigenvalues),
-            (interface_k_hbm, interface_k),
-            (interface_m_hbm, interface_m),
-        ))
+        for n, (whole, held) in enumerate(((eigenvalues_hbm, eigenvalues),))
     ]
     loads = routing + loads + late
     loads.append(pltpu.make_async_copy(modes.at[0], all_modes.at[slab], modes_recv.at[slab]))
@@ -224,7 +215,7 @@
                 def _():
                     arrived[sub] = blocks[step, slab]
 
-    total = [[interface_k[q] for q in range(owned)], [interface_m[q] for q in range(owned)]]
+    total = [[jnp.zeros((quarter, width), jnp.float32)] * owned for _ in range(2)]
     for other in range(subs):
 
         @pl.when((other != sub) | (home != slab))
@@ -238,8 +229,8 @@
             for q in range(owned):
                 total[kind][q] = total[kind][q] + jnp.where(takes[other][q] > 0, term, 0.0)
     for q in range(owned):
-        reduced_k[q] = total[0][q]
-        reduced_m[q] = total[1][q]
+        gram[0, q] = total[0][q]
+        gram[1, q] = total[1][q]
 
     for copy in sends:
         copy.wait_send()
@@ -271,19 +262,16 @@
     group = subs // slabs
     vmem = pl.BlockSpec(memory_space=pltpu.VMEM)
     hbm = pl.BlockSpec(memory_space=pltpu.HBM)
-    out = jax.ShapeDtypeStruct(interface_k.shape, interface_k.dtype)
-    return pl.pallas_call(
+    gram = pl.pallas_call(
         functools.partial(kernel, subs, slabs),
-        out_shape=(out, out),
-        in_specs=[hbm] * 9,
-        out_specs=(vmem, vmem),
+        out_shape=jax.ShapeDtypeStruct((2,) + interface_k.shape, jnp.float32),
+        in_specs=[hbm] * 7,
+        out_specs=vmem,
         scratch_shapes=[
             pltpu.SMEM(adjacency.shape, adjacency.dtype),
             pltpu.SMEM(piece_slot.shape, piece_slot.dtype),
             pltpu.SMEM(tile_range.shape, tile_range.dtype),
             pltpu.VMEM(eigenvalues.shape, eigenvalues.dtype),
-            pltpu.VMEM(interface_k.shape, interface_k.dtype),
-            pltpu.VMEM(interface_m.shape, interface_m.dtype),
             pltpu.VMEM((adj, rows, width), jnp.bfloat16),
             pltpu.VMEM((adj, rows, width), jnp.bfloat16),
             pltpu.VMEM((group, slabs - 1, rows, 2 * width), jnp.bfloat16),
@@ -291,7 +279,7 @@
             pltpu.VMEM((slabs, rows, mode_count), jnp.bfloat16),
             pltpu.VMEM((group, slabs, 2, quarter, width), jnp.bfloat16),
             pltpu.VMEM((subs, 2, quarter, width), jnp.bfloat16),
-            pltpu.SemaphoreType.DMA((6,)),
+            pltpu.SemaphoreType.DMA((4,)),
             pltpu.SemaphoreType.DMA((2, adj)),
             pltpu.SemaphoreType.DMA((slabs - 1,)),
             pltpu.SemaphoreType.DMA((slabs,)),
@@ -311,9 +299,8 @@
         mode_shapes,
         coupling_k,
         coupling_m,
-        interface_k,
-        interface_m,
     )
+    return (interface_k + gram[0], interface_m + gram[1])
 
 
 def sparse_body(

time: 22.2 us -> 21.6 us (0.973)
  local copies, waits for them, and re-layouts: 2 us -> 0 us
  other arithmetic: 0 us -> 1.44 us
    unnamed x4 -> x0, local copies, waits for them, and re-layouts: 2 us -> none
    add x0 -> x1, other arithmetic: none -> 1.44 us  [dense_body(): return (interface_k + gram[0], interface_m + gram[1])]
where the time goes in v3:
time: 21.6 us; the launch traced here: 21.3 us
  Pallas kernels  19.2 us (89%)
  other arithmetic  1.44 us (7%)
  between operations  0.64 us (3%)
    pallas_call x1, Pallas kernels, dense_body(): pl.pallas_call(functools.partial(kernel, subs, slabs), out_shape=jax.Shap...  19.2 us
    add x1, other arithmetic, dense_body(): return (interface_k + gram[0], interface_m + gram[1])  1.44 us

profile of v3, /device:TPU:0, one launch (start us, length us, event | category | flops | bytes accessed | tf_op | source)
XLA Modules:
  0.0 21.3 jit_solution(10270164673413586508)
XLA Ops:
  0.6 19.2 %shard_map.104 = f32[2,2,32,128]{3,2,1,0:T(8,128)} custom-call(s32[8,8]{1,0:T(8,128)} %adjacency_hbm.1, s32[16]{0:T(128)} %piece_slot_hbm.1, s32[1,2,8]{2,1,0:T(2,128)} %tile_range_hbm.1, f32[1,64]{1,0:T(1,128)} %eigenvalues_hbm.1, bf16[1,64,64]{2,1,0:T(8,128)(2,1)} %modes.1, bf16[1,64,1024]{2,1,0:T(8,128)(2,1)} %coupling_k.1, bf16[1,64,1024]{2,1,0:T(8,128)(2,1)} %coupling_m.1), custom_call_target="tpu_custom_call" | custom-call | tf_op jit(solution)/shard_map/pallas_call | solution.py:265
  19.9 1.4 %bitcast_add_fusion = (f32[2,32,128]{2,1,0:T(8,128)}, f32[2,32,128]{2,1,0:T(8,128)}) fusion(f32[2,32,128]{2,1,0:T(8,128)} %param.17, f32[2,2,32,128]{3,2,1,0:T(8,128)} %shard_map.104, f32[2,32,128]{2,1,0:T(8,128)} %param.16), kind=kLoop, calls=%fused_computation | loop fusion | flops 16384 | bytes 196608 | tf_op jit(solution)/shard_map/add | solution.py:303

commit v4 on v3

--- a/solution.py
+++ b/solution.py
@@ -31,6 +31,7 @@
     piece_slot,
     tile_range,
     eigenvalues,
+    my_modes,
     tile_k,
     tile_m,
     outgoing,
@@ -72,9 +73,8 @@
         pltpu.make_async_copy(whole, held, small_sem.at[3 + n])
         for n, (whole, held) in enumerate(((eigenvalues_hbm, eigenvalues),))
     ]
-    loads = routing + loads + late
-    loads.append(pltpu.make_async_copy(modes.at[0], all_modes.at[slab], modes_recv.at[slab]))
-    for load in loads:
+    late.append(pltpu.make_async_copy(modes.at[0], my_modes, small_sem.at[4]))
+    for load in routing + late[1:] + loads:
         load.start()
 
     barrier = pltpu.get_barrier_semaphore()
@@ -91,6 +91,10 @@
     def _():
         pl.semaphore_signal(barrier, inc=1, device_id=(sub, home), device_id_type=MESH)
 
+    late[0].start()
+    late[1].wait()
+    half = rows // 2
+    all_modes[slab] = jnp.concatenate([my_modes[:half], my_modes[half:]], axis=1)
     for load in routing:
         load.wait()
     slots = [piece_slot[adjacency[sub, a]] for a in range(adj)]
@@ -98,29 +102,31 @@
     def owner_of(part, step):
         return part * group + lax.rem(step + sub + 1, group)
 
-    for load in loads[len(routing) : -1 - len(late)]:
-        load.wait()
-    row_index = slab * rows + lax.broadcasted_iota(jnp.int32, (rows, width), 0)
-    for turn in list(range(1, slabs)) + [0]:
-        part = lax.rem(slab + turn, slabs)
-        for step in range(group):
-            owner = owner_of(part, step)
+    plan = []
+    for step in range(group):
+        for turn in list(range(1, slabs)) + [0]:
+            owner = owner_of(lax.rem(slab + turn, slabs), step)
             place = jnp.int32(0)
             for a in range(adj):
                 mine = (slots[a] >= owner * owned) & (slots[a] < (owner + 1) * owned)
                 place = jnp.where(mine, jnp.int32(a), place)
-            start = tile_range[0, 0, place]
-            finish = tile_range[0, 1, place]
-            live = ((row_index >= start) & (row_index < finish)).astype(jnp.float32)
-            live = live.astype(jnp.bfloat16)
-            stiff = tile_k[place] * live
-            mass = tile_m[place] * live
-            if turn == 0:
-                columns[step, slab, :, 0:width] = stiff
-                columns[step, slab, :, width:] = mass
-            else:
-                outgoing[step, turn - 1, :, 0:width] = stiff
-                outgoing[step, turn - 1, :, width:] = mass
+            start = tile_range[0, 0, place] - slab * rows
+            finish = tile_range[0, 1, place] - slab * rows
+            plan.append((step, turn, place, start, finish))
+    row_index = lax.broadcasted_iota(jnp.int32, (rows, width), 0)
+    for load in loads:
+        load.wait()
+    for step, turn, place, start, finish in plan:
+        live = ((row_index >= start) & (row_index < finish)).astype(jnp.float32)
+        live = live.astype(jnp.bfloat16)
+        stiff = tile_k[place] * live
+        mass = tile_m[place] * live
+        if turn == 0:
+            columns[step, slab, :, 0:width] = stiff
+            columns[step, slab, :, width:] = mass
+        else:
+            outgoing[step, turn - 1, :, 0:width] = stiff
+            outgoing[step, turn - 1, :, width:] = mass
 
     @pl.when(home != slab)
     def _():
@@ -134,7 +140,7 @@
     for turn in range(1, slabs):
         part = lax.rem(slab + turn, slabs)
         copy = pltpu.make_async_remote_copy(
-            src_ref=modes.at[0],
+            src_ref=all_modes.at[slab],
             dst_ref=all_modes.at[slab],
             send_sem=modes_send.at[turn - 1],
             recv_sem=modes_recv.at[slab],
@@ -167,23 +173,30 @@
             )
             for q in range(owned)
         ])
-    for load in late:
-        load.wait()
+    late[0].wait()
     eig = jnp.broadcast_to(eigenvalues[...], (width, modes.shape[2])).T
     root = lax.rsqrt(eig)
 
-    loads[-1].wait()
     for turn in range(1, slabs):
         part = lax.rem(slab + turn, slabs)
         pltpu.make_async_copy(all_modes.at[part], all_modes.at[part], modes_recv.at[part]).wait()
-    basis = all_modes[...].reshape(slabs * rows, modes.shape[2])
+    mode_count = modes.shape[2]
+    basis = jnp.concatenate([
+        all_modes[part, :, side * mode_count : (side + 1) * mode_count]
+        for part in range(slabs)
+        for side in range(2)
+    ]).T
     for step in range(group):
         for turn in range(1, slabs):
             part = lax.rem(slab + turn, slabs)
             pltpu.make_async_copy(
                 columns.at[step, part], columns.at[step, part], columns_recv.at[step, part]
             ).wait()
-        proj = contract_rows(basis, columns[step].reshape(slabs * rows, 2 * width))
+        proj = jnp.dot(
+            basis,
+            columns[step].reshape(slabs * rows, 2 * width),
+            preferred_element_type=jnp.float32,
+        )
         proj_s, proj_v = proj[:, :width], proj[:, width:]
         first = (proj_s * root).astype(jnp.bfloat16)
         second = (proj_s / eig - proj_v).astype(jnp.bfloat16)
@@ -215,6 +228,16 @@
                 def _():
                     arrived[sub] = blocks[step, slab]
 
+    for copy in sends:
+        copy.wait_send()
+    for step in range(group):
+
+        @pl.when(owner_of(slab, step) != sub)
+        def _():
+            pltpu.make_async_copy(
+                blocks.at[step, slab], blocks.at[step, slab], blocks_send.at[step, slabs - 1]
+            ).wait()
+
     total = [[jnp.zeros((quarter, width), jnp.float32)] * owned for _ in range(2)]
     for other in range(subs):
 
@@ -231,16 +254,6 @@
     for q in range(owned):
         gram[0, q] = total[0][q]
         gram[1, q] = total[1][q]
-
-    for copy in sends:
-        copy.wait_send()
-    for step in range(group):
-
-        @pl.when(owner_of(slab, step) != sub)
-        def _():
-            pltpu.make_async_copy(
-                blocks.at[step, slab], blocks.at[step, slab], blocks_send.at[step, slabs - 1]
-            ).wait()
 
 
 def dense_body(
@@ -272,14 +285,15 @@
             pltpu.SMEM(piece_slot.shape, piece_slot.dtype),
             pltpu.SMEM(tile_range.shape, tile_range.dtype),
             pltpu.VMEM(eigenvalues.shape, eigenvalues.dtype),
+            pltpu.VMEM((rows, mode_count), jnp.bfloat16),
             pltpu.VMEM((adj, rows, width), jnp.bfloat16),
             pltpu.VMEM((adj, rows, width), jnp.bfloat16),
             pltpu.VMEM((group, slabs - 1, rows, 2 * width), jnp.bfloat16),
             pltpu.VMEM((group, slabs, rows, 2 * width), jnp.bfloat16),
-            pltpu.VMEM((slabs, rows, mode_count), jnp.bfloat16),
+            pltpu.VMEM((slabs, rows // 2, 2 * mode_count), jnp.bfloat16),
             pltpu.VMEM((group, slabs, 2, quarter, width), jnp.bfloat16),
             pltpu.VMEM((subs, 2, quarter, width), jnp.bfloat16),
-            pltpu.SemaphoreType.DMA((4,)),
+            pltpu.SemaphoreType.DMA((5,)),
             pltpu.SemaphoreType.DMA((2, adj)),
             pltpu.SemaphoreType.DMA((slabs - 1,)),
             pltpu.SemaphoreType.DMA((slabs,)),
@@ -289,7 +303,7 @@
             pltpu.SemaphoreType.DMA((subs,)),
         ],
         compiler_params=pltpu.CompilerParams(
-            collective_id=0, has_side_effects=True, vmem_limit_bytes=64 * 1024 * 1024
+            collective_id=0, has_side_effects=True, vmem_limit_bytes=56 * 1024 * 1024
         ),
     )(
         adjacency,

time: 21.6 us -> 21 us (0.972)
  Pallas kernels: 19.2 us -> 18.6 us
    pallas_call x1, Pallas kernels: 19.2 us -> 18.6 us  [dense_body(): pl.pallas_call(functools.partial(kernel, subs, slabs), out_shape=jax.Shap...]
where the time goes in v4:
time: 21 us; the launch traced here: 20.7 us
  Pallas kernels  18.6 us (89%)
  other arithmetic  1.41 us (7%)
  between operations  0.67 us (3%)
    pallas_call x1, Pallas kernels, dense_body(): pl.pallas_call(functools.partial(kernel, subs, slabs), out_shape=jax.Shap...  18.6 us
    add x1, other arithmetic, dense_body(): return (interface_k + gram[0], interface_m + gram[1])  1.41 us

profile of v4, /device:TPU:0, one launch (start us, length us, event | category | flops | bytes accessed | tf_op | source)
XLA Modules:
  0.0 20.7 jit_solution(14690239988303371481)
XLA Ops:
  0.6 0.0 copy-start
  0.6 0.0 copy-start.1
  0.7 18.6 %shard_map.104 = f32[2,2,32,128]{3,2,1,0:T(8,128)} custom-call(s32[8,8]{1,0:T(8,128)} %adjacency_hbm.1, s32[16]{0:T(128)} %piece_slot_hbm.1, s32[1,2,8]{2,1,0:T(2,128)} %tile_range_hbm.1, f32[1,64]{1,0:T(1,128)} %eigenvalues_hbm.1, bf16[1,64,64]{2,1,0:T(8,128)(2,1)} %modes.1, bf16[1,64,1024]{2,1,0:T(8,128)(2,1)} %coupling_k.1, bf16[1,64,1024]{2,1,0:T(8,128)(2,1)} %coupling_m.1), custom_call_target="tpu_custom_call" | custom-call | tf_op jit(solution)/shard_map/pallas_call | solution.py:278
  19.3 0.0 copy-done
  19.3 0.0 copy-done.1
  19.3 1.4 %bitcast_add_fusion = (f32[2,32,128]{2,1,0:T(8,128)}, f32[2,32,128]{2,1,0:T(8,128)}) fusion(f32[2,32,128]{2,1,0:T(8,128)S(1)} %copy-done, f32[2,2,32,128]{3,2,1,0:T(8,128)} %shard_map.104, f32[2,32,128]{2,1,0:T(8,128)S(1)} %copy-done.1), kind=kLoop, calls=%fused_computation | loop fusion | flops 16384 | bytes 196608 | tf_op jit(solution)/shard_map/add | solution.py:317
Async XLA Ops:
  0.6 18.7 %copy-start = (f32[2,32,128]{2,1,0:T(8,128)S(1)}, f32[2,32,128]{2,1,0:T(8,128)}, u32[]{:S(2)}) copy-start(f32[2,32,128]{2,1,0:T(8,128)} %param.17) | copy-start | bytes 98308
  0.6 18.7 %copy-start.1 = (f32[2,32,128]{2,1,0:T(8,128)S(1)}, f32[2,32,128]{2,1,0:T(8,128)}, u32[]{:S(2)}) copy-start(f32[2,32,128]{2,1,0:T(8,128)} %param.16) | copy-start | bytes 98308

commit v5 on v4

--- a/solution.py
+++ b/solution.py
@@ -114,19 +114,36 @@
             finish = tile_range[0, 1, place] - slab * rows
             plan.append((step, turn, place, start, finish))
     row_index = lax.broadcasted_iota(jnp.int32, (rows, width), 0)
+    live = {}
+    for step, turn, place, start, finish in plan:
+        inside = (row_index >= start) & (row_index < finish)
+        live[step, turn] = inside.astype(jnp.float32).astype(jnp.bfloat16)
     for load in loads:
         load.wait()
-    for step, turn, place, start, finish in plan:
-        live = ((row_index >= start) & (row_index < finish)).astype(jnp.float32)
-        live = live.astype(jnp.bfloat16)
-        stiff = tile_k[place] * live
-        mass = tile_m[place] * live
-        if turn == 0:
-            columns[step, slab, :, 0:width] = stiff
-            columns[step, slab, :, width:] = mass
-        else:
-            outgoing[step, turn - 1, :, 0:width] = stiff
-            outgoing[step, turn - 1, :, width:] = mass
+
+    def stage(wanted, kind):
+        tile = (tile_k, tile_m)[kind]
+        for step, turn, place, _, _ in plan:
+            if step == wanted and turn > 0:
+                outgoing[step, kind, turn - 1] = tile[place] * live[step, turn]
+
+    sends = []
+
+    def send_columns(step, kind):
+        for turn in range(1, slabs):
+            part = lax.rem(slab + turn, slabs)
+            copy = pltpu.make_async_remote_copy(
+                src_ref=outgoing.at[step, kind, turn - 1],
+                dst_ref=columns.at[step, kind, slab],
+                send_sem=columns_send.at[step, kind, turn - 1],
+                recv_sem=columns_recv.at[step, kind, slab],
+                device_id=(sub, part),
+                device_id_type=MESH,
+            )
+            copy.start()
+            sends.append(copy)
+
+    stage(0, 0)
 
     @pl.when(home != slab)
     def _():
@@ -136,7 +153,6 @@
     def _():
         pl.semaphore_wait(barrier, slabs - 1 + group * slabs - 1)
 
-    sends = []
     for turn in range(1, slabs):
         part = lax.rem(slab + turn, slabs)
         copy = pltpu.make_async_remote_copy(
@@ -149,19 +165,16 @@
         )
         copy.start()
         sends.append(copy)
+    send_columns(0, 0)
     for step in range(group):
-        for turn in range(1, slabs):
-            part = lax.rem(slab + turn, slabs)
-            copy = pltpu.make_async_remote_copy(
-                src_ref=outgoing.at[step, turn - 1],
-                dst_ref=columns.at[step, slab],
-                send_sem=columns_send.at[step, turn - 1],
-                recv_sem=columns_recv.at[step, slab],
-                device_id=(sub, part),
-                device_id_type=MESH,
-            )
-            copy.start()
-            sends.append(copy)
+        for kind in range(2):
+            if step + kind > 0:
+                stage(step, kind)
+                send_columns(step, kind)
+    for step, turn, place, _, _ in plan:
+        if turn == 0:
+            columns[step, 0, slab] = tile_k[place] * live[step, 0]
+            columns[step, 1, slab] = tile_m[place] * live[step, 0]
 
     takes = []
     for other in range(subs):
@@ -187,46 +200,51 @@
         for side in range(2)
     ]).T
     for step in range(group):
-        for turn in range(1, slabs):
-            part = lax.rem(slab + turn, slabs)
-            pltpu.make_async_copy(
-                columns.at[step, part], columns.at[step, part], columns_recv.at[step, part]
-            ).wait()
-        proj = jnp.dot(
-            basis,
-            columns[step].reshape(slabs * rows, 2 * width),
-            preferred_element_type=jnp.float32,
-        )
-        proj_s, proj_v = proj[:, :width], proj[:, width:]
-        first = (proj_s * root).astype(jnp.bfloat16)
-        second = (proj_s / eig - proj_v).astype(jnp.bfloat16)
-        third = proj_v.astype(jnp.bfloat16)
-        gram_k = contract_rows(first, first)
-        gram_m = contract_rows(
-            jnp.concatenate([second, third]), jnp.concatenate([second, -third])
-        )
-        blocks[step, :, 0] = gram_k.astype(jnp.bfloat16).reshape(slabs, quarter, width)
-        blocks[step, :, 1] = gram_m.astype(jnp.bfloat16).reshape(slabs, quarter, width)
         owner = owner_of(slab, step)
-        for turn in range(1, slabs + 1):
-            part = lax.rem(slab + turn, slabs)
-            copy = pltpu.make_async_remote_copy(
-                src_ref=blocks.at[step, part],
-                dst_ref=arrived.at[sub],
-                send_sem=blocks_send.at[step, turn - 1],
-                recv_sem=blocks_recv.at[sub],
-                device_id=(owner, part),
-                device_id_type=MESH,
+        for kind in range(2):
+            for turn in range(1, slabs):
+                part = lax.rem(slab + turn, slabs)
+                pltpu.make_async_copy(
+                    columns.at[step, kind, part],
+                    columns.at[step, kind, part],
+                    columns_recv.at[step, kind, part],
+                ).wait()
+            proj = jnp.dot(
+                basis,
+                columns[step, kind].reshape(slabs * rows, width),
+                preferred_element_type=jnp.float32,
             )
-            if turn < slabs:
-                copy.start()
-                sends.append(copy)
+            if kind == 0:
+                proj_s = proj
+                first = (proj_s * root).astype(jnp.bfloat16)
+                gram_part = contract_rows(first, first)
             else:
-                pl.when(owner != sub)(copy.start)
-
-                @pl.when(owner == sub)
-                def _():
-                    arrived[sub] = blocks[step, slab]
+                second = (proj_s / eig - proj).astype(jnp.bfloat16)
+                third = proj.astype(jnp.bfloat16)
+                gram_part = contract_rows(
+                    jnp.concatenate([second, third]), jnp.concatenate([second, -third])
+                )
+            blocks[step, kind] = gram_part.astype(jnp.bfloat16).reshape(slabs, quarter, width)
+            for turn in range(1, slabs + 1):
+                part = lax.rem(slab + turn, slabs)
+                copy = pltpu.make_async_remote_copy(
+                    src_ref=blocks.at[step, kind, part],
+                    dst_ref=arrived.at[sub, kind],
+                    send_sem=blocks_send.at[step, kind, turn - 1],
+                    recv_sem=blocks_recv.at[sub, kind],
+                    device_id=(owner, part),
+                    device_id_type=MESH,
+                )
+                if turn < slabs:
+                    copy.start()
+                    sends.append(copy)
+                else:
+                    pl.when(owner != sub)(copy.start)
+
+        @pl.when(owner == sub)
+        def _():
+            for kind in range(2):
+                arrived[sub, kind] = blocks[step, kind, slab]
 
     for copy in sends:
         copy.wait_send()
@@ -234,18 +252,18 @@
 
         @pl.when(owner_of(slab, step) != sub)
         def _():
-            pltpu.make_async_copy(
-                blocks.at[step, slab], blocks.at[step, slab], blocks_send.at[step, slabs - 1]
-            ).wait()
+            for kind in range(2):
+                mine = blocks.at[step, kind, slab]
+                pltpu.make_async_copy(mine, mine, blocks_send.at[step, kind, slabs - 1]).wait()
 
     total = [[jnp.zeros((quarter, width), jnp.float32)] * owned for _ in range(2)]
     for other in range(subs):
 
         @pl.when((other != sub) | (home != slab))
         def _():
-            pltpu.make_async_copy(
-                arrived.at[other], arrived.at[other], blocks_recv.at[other]
-            ).wait()
+            for kind in range(2):
+                theirs = arrived.at[other, kind]
+                pltpu.make_async_copy(theirs, theirs, blocks_recv.at[other, kind]).wait()
 
         for kind in range(2):
             term = arrived[other, kind].astype(jnp.float32)
@@ -288,19 +306,19 @@
             pltpu.VMEM((rows, mode_count), jnp.bfloat16),
             pltpu.VMEM((adj, rows, width), jnp.bfloat16),
             pltpu.VMEM((adj, rows, width), jnp.bfloat16),
-            pltpu.VMEM((group, slabs - 1, rows, 2 * width), jnp.bfloat16),
-            pltpu.VMEM((group, slabs, rows, 2 * width), jnp.bfloat16),
+            pltpu.VMEM((group, 2, slabs - 1, rows, width), jnp.bfloat16),
+            pltpu.VMEM((group, 2, slabs, rows, width), jnp.bfloat16),
             pltpu.VMEM((slabs, rows // 2, 2 * mode_count), jnp.bfloat16),
-            pltpu.VMEM((group, slabs, 2, quarter, width), jnp.bfloat16),
+            pltpu.VMEM((group, 2, slabs, quarter, width), jnp.bfloat16),
             pltpu.VMEM((subs, 2, quarter, width), jnp.bfloat16),
             pltpu.SemaphoreType.DMA((5,)),
             pltpu.SemaphoreType.DMA((2, adj)),
             pltpu.SemaphoreType.DMA((slabs - 1,)),
             pltpu.SemaphoreType.DMA((slabs,)),
-            pltpu.SemaphoreType.DMA((group, slabs - 1)),
-            pltpu.SemaphoreType.DMA((group, slabs)),
-            pltpu.SemaphoreType.DMA((group, slabs)),
-            pltpu.SemaphoreType.DMA((subs,)),
+            pltpu.SemaphoreType.DMA((group, 2, slabs - 1)),
+            pltpu.SemaphoreType.DMA((group, 2, slabs)),
+            pltpu.SemaphoreType.DMA((group, 2, slabs)),
+            pltpu.SemaphoreType.DMA((subs, 2)),
         ],
         compiler_params=pltpu.CompilerParams(
             collective_id=0, has_side_effects=True, vmem_limit_bytes=56 * 1024 * 1024

time: 21 us -> 20.6 us (0.981)
  Pallas kernels: 18.6 us -> 18.2 us
    pallas_call x1, Pallas kernels: 18.6 us -> 18.2 us  [dense_body(): pl.pallas_call(functools.partial(kernel, subs, slabs), out_shape=jax.Shap...]
where the time goes in v5:
time: 20.6 us; the launch traced here: 20.3 us
  Pallas kernels  18.2 us (88%)
  other arithmetic  1.41 us (7%)
  between operations  0.67 us (3%)
    pallas_call x1, Pallas kernels, dense_body(): pl.pallas_call(functools.partial(kernel, subs, slabs), out_shape=jax.Shap...  18.2 us
    add x1, other arithmetic, dense_body(): return (interface_k + gram[0], interface_m + gram[1])  1.41 us

profile of v5, /device:TPU:0, one launch (start us, length us, event | category | flops | bytes accessed | tf_op | source)
XLA Modules:
  0.0 20.3 jit_solution(8705356429694974229)
XLA Ops:
  0.6 0.0 copy-start
  0.6 0.0 copy-start.1
  0.7 18.2 %shard_map.104 = f32[2,2,32,128]{3,2,1,0:T(8,128)} custom-call(s32[8,8]{1,0:T(8,128)} %adjacency_hbm.1, s32[16]{0:T(128)} %piece_slot_hbm.1, s32[1,2,8]{2,1,0:T(2,128)} %tile_range_hbm.1, f32[1,64]{1,0:T(1,128)} %eigenvalues_hbm.1, bf16[1,64,64]{2,1,0:T(8,128)(2,1)} %modes.1, bf16[1,64,1024]{2,1,0:T(8,128)(2,1)} %coupling_k.1, bf16[1,64,1024]{2,1,0:T(8,128)(2,1)} %coupling_m.1), custom_call_target="tpu_custom_call" | custom-call | tf_op jit(solution)/shard_map/pallas_call | solution.py:296
  18.9 0.0 copy-done
  18.9 0.0 copy-done.1
  18.9 1.4 %bitcast_add_fusion = (f32[2,32,128]{2,1,0:T(8,128)}, f32[2,32,128]{2,1,0:T(8,128)}) fusion(f32[2,32,128]{2,1,0:T(8,128)S(1)} %copy-done, f32[2,2,32,128]{3,2,1,0:T(8,128)} %shard_map.104, f32[2,32,128]{2,1,0:T(8,128)S(1)} %copy-done.1), kind=kLoop, calls=%fused_computation | loop fusion | flops 16384 | bytes 196608 | tf_op jit(solution)/shard_map/add | solution.py:335
Async XLA Ops:
  0.6 18.2 %copy-start = (f32[2,32,128]{2,1,0:T(8,128)S(1)}, f32[2,32,128]{2,1,0:T(8,128)}, u32[]{:S(2)}) copy-start(f32[2,32,128]{2,1,0:T(8,128)} %param.17) | copy-start | bytes 98308
  0.6 18.2 %copy-start.1 = (f32[2,32,128]{2,1,0:T(8,128)S(1)}, f32[2,32,128]{2,1,0:T(8,128)}, u32[]{:S(2)}) copy-start(f32[2,32,128]{2,1,0:T(8,128)} %param.16) | copy-start | bytes 98308

commit v6 on v5

--- a/solution.py
+++ b/solution.py
@@ -295,7 +295,7 @@
     hbm = pl.BlockSpec(memory_space=pltpu.HBM)
     gram = pl.pallas_call(
         functools.partial(kernel, subs, slabs),
-        out_shape=jax.ShapeDtypeStruct((2,) + interface_k.shape, jnp.float32),
+        out_shape=pltpu.VMEM((2,) + interface_k.shape, jnp.float32),
         in_specs=[hbm] * 7,
         out_specs=vmem,
         scratch_shapes=[

time: 20.6 us -> 19.1 us (0.927)
  other arithmetic: 1.41 us -> 0.63 us
  Pallas kernels: 18.2 us -> 17.6 us
    add x1, other arithmetic: 1.41 us -> 0.63 us  [dense_body(): return (interface_k + gram[0], interface_m + gram[1])]
    pallas_call x1, Pallas kernels: 18.2 us -> 17.6 us  [dense_body(): pl.pallas_call(functools.partial(kernel, subs, slabs), out_shape=pltpu.VM...]
where the time goes in v6:
time: 19.1 us; the launch traced here: 18.9 us
  Pallas kernels  17.6 us (92%)
  between operations  0.67 us (4%)
  other arithmetic  0.63 us (3%)
    pallas_call x1, Pallas kernels, dense_body(): pl.pallas_call(functools.partial(kernel, subs, slabs), out_shape=pltpu.VM...  17.6 us
    add x1, other arithmetic, dense_body(): return (interface_k + gram[0], interface_m + gram[1])  0.63 us

profile of v6, /device:TPU:0, one launch (start us, length us, event | category | flops | bytes accessed | tf_op | source)
XLA Modules:
  0.0 18.9 jit_solution(14596068400036545780)
XLA Ops:
  0.6 0.0 copy-start
  0.6 0.0 copy-start.1
  0.7 17.6 %shard_map.104 = f32[2,2,32,128]{3,2,1,0:T(8,128)S(1)} custom-call(s32[8,8]{1,0:T(8,128)} %adjacency_hbm.1, s32[16]{0:T(128)} %piece_slot_hbm.1, s32[1,2,8]{2,1,0:T(2,128)} %tile_range_hbm.1, f32[1,64]{1,0:T(1,128)} %eigenvalues_hbm.1, bf16[1,64,64]{2,1,0:T(8,128)(2,1)} %modes.1, bf16[1,64,1024]{2,1,0:T(8,128)(2,1)} %coupling_k.1, ...), custom_call_target="tpu_custom_call" | custom-call | tf_op jit(solution)/shard_map/pallas_call | solution.py:296
  18.3 0.0 copy-done
  18.3 0.0 copy-done.1
  18.3 0.6 %bitcast_add_fusion = (f32[2,32,128]{2,1,0:T(8,128)}, f32[2,32,128]{2,1,0:T(8,128)}) fusion(f32[2,32,128]{2,1,0:T(8,128)S(1)} %copy-done, f32[2,2,32,128]{3,2,1,0:T(8,128)S(1)} %shard_map.104, f32[2,32,128]{2,1,0:T(8,128)S(1)} %copy-done.1), kind=kLoop, calls=%fused_computation | loop fusion | flops 16384 | bytes 196608 | tf_op jit(solution)/shard_map/add | solution.py:335
Async XLA Ops:
  0.6 17.6 %copy-start = (f32[2,32,128]{2,1,0:T(8,128)S(1)}, f32[2,32,128]{2,1,0:T(8,128)}, u32[]{:S(2)}) copy-start(f32[2,32,128]{2,1,0:T(8,128)} %param.17) | copy-start | bytes 98308
  0.6 17.6 %copy-start.1 = (f32[2,32,128]{2,1,0:T(8,128)S(1)}, f32[2,32,128]{2,1,0:T(8,128)}, u32[]{:S(2)}) copy-start(f32[2,32,128]{2,1,0:T(8,128)} %param.16) | copy-start | bytes 98308

commit v7 on v6

--- a/solution.py
+++ b/solution.py
@@ -56,11 +56,13 @@
     rows = modes.shape[1]
     home = sub // group
 
-    loads = [
-        pltpu.make_async_copy(
-            whole.at[0, :, a * width : (a + 1) * width], tile.at[a], local_sem.at[kind, a]
-        )
-        for a in range(adj)
+    loads_k, loads_m = [
+        [
+            pltpu.make_async_copy(
+                whole.at[0, :, a * width : (a + 1) * width], tile.at[a], local_sem.at[kind, a]
+            )
+            for a in range(adj)
+        ]
         for kind, (whole, tile) in enumerate(((coupling_k, tile_k), (coupling_m, tile_m)))
     ]
     routing = [
@@ -74,7 +76,7 @@
         for n, (whole, held) in enumerate(((eigenvalues_hbm, eigenvalues),))
     ]
     late.append(pltpu.make_async_copy(modes.at[0], my_modes, small_sem.at[4]))
-    for load in routing + late[1:] + loads:
+    for load in routing + loads_k + late[1:]:
         load.start()
 
     barrier = pltpu.get_barrier_semaphore()
@@ -91,10 +93,8 @@
     def _():
         pl.semaphore_signal(barrier, inc=1, device_id=(sub, home), device_id_type=MESH)
 
-    late[0].start()
-    late[1].wait()
-    half = rows // 2
-    all_modes[slab] = jnp.concatenate([my_modes[:half], my_modes[half:]], axis=1)
+    for load in loads_m + late[:1]:
+        load.start()
     for load in routing:
         load.wait()
     slots = [piece_slot[adjacency[sub, a]] for a in range(adj)]
@@ -118,7 +118,7 @@
     for step, turn, place, start, finish in plan:
         inside = (row_index >= start) & (row_index < finish)
         live[step, turn] = inside.astype(jnp.float32).astype(jnp.bfloat16)
-    for load in loads:
+    for load in loads_k:
         load.wait()
 
     def stage(wanted, kind):
@@ -144,6 +144,9 @@
             sends.append(copy)
 
     stage(0, 0)
+    late[1].wait()
+    half = rows // 2
+    all_modes[slab] = jnp.concatenate([my_modes[:half], my_modes[half:]], axis=1)
 
     @pl.when(home != slab)
     def _():
@@ -166,6 +169,8 @@
         copy.start()
         sends.append(copy)
     send_columns(0, 0)
+    for load in loads_m:
+        load.wait()
     for step in range(group):
         for kind in range(2):
             if step + kind > 0:
@@ -215,11 +220,11 @@
                 preferred_element_type=jnp.float32,
             )
             if kind == 0:
-                proj_s = proj
-                first = (proj_s * root).astype(jnp.bfloat16)
+                ratio = proj / eig
+                first = (proj * root).astype(jnp.bfloat16)
                 gram_part = contract_rows(first, first)
             else:
-                second = (proj_s / eig - proj).astype(jnp.bfloat16)
+                second = (ratio - proj).astype(jnp.bfloat16)
                 third = proj.astype(jnp.bfloat16)
                 gram_part = contract_rows(
                     jnp.concatenate([second, third]), jnp.concatenate([second, -third])

time: 19.1 us -> 19.1 us (level)
  no operation moved by 1% of the time
where the time goes in v7:
time: 19.1 us; the launch traced here: 18.9 us
  Pallas kernels  17.6 us (92%)
  between operations  0.67 us (4%)
  other arithmetic  0.63 us (3%)
    pallas_call x1, Pallas kernels, dense_body(): pl.pallas_call(functools.partial(kernel, subs, slabs), out_shape=pltpu.VM...  17.6 us
    add x1, other arithmetic, dense_body(): return (interface_k + gram[0], interface_m + gram[1])  0.63 us

profile of v7, /device:TPU:0, one launch (start us, length us, event | category | flops | bytes accessed | tf_op | source)
XLA Modules:
  0.0 18.9 jit_solution(14664182276088196993)
XLA Ops:
  0.6 0.0 copy-start
  0.6 0.0 copy-start.1
  0.7 17.6 %shard_map.104 = f32[2,2,32,128]{3,2,1,0:T(8,128)S(1)} custom-call(s32[8,8]{1,0:T(8,128)} %adjacency_hbm.1, s32[16]{0:T(128)} %piece_slot_hbm.1, s32[1,2,8]{2,1,0:T(2,128)} %tile_range_hbm.1, f32[1,64]{1,0:T(1,128)} %eigenvalues_hbm.1, bf16[1,64,64]{2,1,0:T(8,128)(2,1)} %modes.1, bf16[1,64,1024]{2,1,0:T(8,128)(2,1)} %coupling_k.1, ...), custom_call_target="tpu_custom_call" | custom-call | tf_op jit(solution)/shard_map/pallas_call | solution.py:301
  18.3 0.0 copy-done
  18.3 0.0 copy-done.1
  18.3 0.6 %bitcast_add_fusion = (f32[2,32,128]{2,1,0:T(8,128)}, f32[2,32,128]{2,1,0:T(8,128)}) fusion(f32[2,32,128]{2,1,0:T(8,128)S(1)} %copy-done, f32[2,2,32,128]{3,2,1,0:T(8,128)S(1)} %shard_map.104, f32[2,32,128]{2,1,0:T(8,128)S(1)} %copy-done.1), kind=kLoop, calls=%fused_computation | loop fusion | flops 16384 | bytes 196608 | tf_op jit(solution)/shard_map/add | solution.py:340
Async XLA Ops:
  0.6 17.6 %copy-start = (f32[2,32,128]{2,1,0:T(8,128)S(1)}, f32[2,32,128]{2,1,0:T(8,128)}, u32[]{:S(2)}) copy-start(f32[2,32,128]{2,1,0:T(8,128)} %param.17) | copy-start | bytes 98308
  0.6 17.6 %copy-start.1 = (f32[2,32,128]{2,1,0:T(8,128)S(1)}, f32[2,32,128]{2,1,0:T(8,128)}, u32[]{:S(2)}) copy-start(f32[2,32,128]{2,1,0:T(8,128)} %param.16) | copy-start | bytes 98308

commit v8 on v7

--- a/solution.py
+++ b/solution.py
@@ -171,11 +171,11 @@
     send_columns(0, 0)
     for load in loads_m:
         load.wait()
-    for step in range(group):
-        for kind in range(2):
-            if step + kind > 0:
-                stage(step, kind)
-                send_columns(step, kind)
+    parts = [(step, kind) for step in range(group) for kind in range(2)]
+    stage(*parts[1])
+    send_columns(*parts[1])
+    for part in parts[2:]:
+        stage(*part)
     for step, turn, place, _, _ in plan:
         if turn == 0:
             columns[step, 0, slab] = tile_k[place] * live[step, 0]
@@ -214,6 +214,9 @@
                     columns.at[step, kind, part],
                     columns_recv.at[step, kind, part],
                 ).wait()
+            following = 2 * step + kind + 2
+            if following < len(parts):
+                send_columns(*parts[following])
             proj = jnp.dot(
                 basis,
                 columns[step, kind].reshape(slabs * rows, width),

time: 19.1 us -> 19.5 us (1.021)
  Pallas kernels: 17.6 us -> 18 us
    pallas_call x1, Pallas kernels: 17.6 us -> 18 us  [dense_body(): pl.pallas_call(functools.partial(kernel, subs, slabs), out_shape=pltpu.VM...]
where the time goes in v8:
time: 19.5 us; the launch traced here: 19.3 us
  Pallas kernels  18 us (92%)
  between operations  0.67 us (3%)
  other arithmetic  0.63 us (3%)
    pallas_call x1, Pallas kernels, dense_body(): pl.pallas_call(functools.partial(kernel, subs, slabs), out_shape=pltpu.VM...  18 us
    add x1, other arithmetic, dense_body(): return (interface_k + gram[0], interface_m + gram[1])  0.63 us

profile of v8, /device:TPU:0, one launch (start us, length us, event | category | flops | bytes accessed | tf_op | source)
XLA Modules:
  0.0 19.3 jit_solution(11960227871661900541)
XLA Ops:
  0.6 0.0 copy-start
  0.6 0.0 copy-start.1
  0.7 18.0 %shard_map.104 = f32[2,2,32,128]{3,2,1,0:T(8,128)S(1)} custom-call(s32[8,8]{1,0:T(8,128)} %adjacency_hbm.1, s32[16]{0:T(128)} %piece_slot_hbm.1, s32[1,2,8]{2,1,0:T(2,128)} %tile_range_hbm.1, f32[1,64]{1,0:T(1,128)} %eigenvalues_hbm.1, bf16[1,64,64]{2,1,0:T(8,128)(2,1)} %modes.1, bf16[1,64,1024]{2,1,0:T(8,128)(2,1)} %coupling_k.1, ...), custom_call_target="tpu_custom_call" | custom-call | tf_op jit(solution)/shard_map/pallas_call | solution.py:304
  18.7 0.0 copy-done
  18.7 0.0 copy-done.1
  18.7 0.6 %bitcast_add_fusion = (f32[2,32,128]{2,1,0:T(8,128)}, f32[2,32,128]{2,1,0:T(8,128)}) fusion(f32[2,32,128]{2,1,0:T(8,128)S(1)} %copy-done, f32[2,2,32,128]{3,2,1,0:T(8,128)S(1)} %shard_map.104, f32[2,32,128]{2,1,0:T(8,128)S(1)} %copy-done.1), kind=kLoop, calls=%fused_computation | loop fusion | flops 16384 | bytes 196608 | tf_op jit(solution)/shard_map/add | solution.py:343
Async XLA Ops:
  0.6 18.0 %copy-start = (f32[2,32,128]{2,1,0:T(8,128)S(1)}, f32[2,32,128]{2,1,0:T(8,128)}, u32[]{:S(2)}) copy-start(f32[2,32,128]{2,1,0:T(8,128)} %param.17) | copy-start | bytes 98308
  0.6 18.0 %copy-start.1 = (f32[2,32,128]{2,1,0:T(8,128)S(1)}, f32[2,32,128]{2,1,0:T(8,128)}, u32[]{:S(2)}) copy-start(f32[2,32,128]{2,1,0:T(8,128)} %param.16) | copy-start | bytes 98308

commit v9 on v6

--- a/solution.py
+++ b/solution.py
@@ -54,7 +54,7 @@
     adj = adjacency.shape[1]
     _, owned, quarter, width = gram.shape
     rows = modes.shape[1]
-    home = sub // group
+    home = lax.rem(sub, slabs)
 
     loads = [
         pltpu.make_async_copy(
@@ -100,7 +100,7 @@
     slots = [piece_slot[adjacency[sub, a]] for a in range(adj)]
 
     def owner_of(part, step):
-        return part * group + lax.rem(step + sub + 1, group)
+        return part + slabs * lax.rem(step + sub // slabs + 1, group)
 
     plan = []
     for step in range(group):

time: 19.1 us -> 18.5 us (0.969)
  Pallas kernels: 17.6 us -> 17 us
    pallas_call x1, Pallas kernels: 17.6 us -> 17 us  [dense_body(): pl.pallas_call(functools.partial(kernel, subs, slabs), out_shape=pltpu.VM...]
where the time goes in v9:
time: 18.5 us; the launch traced here: 18.3 us
  Pallas kernels  17 us (92%)
  between operations  0.67 us (4%)
  other arithmetic  0.63 us (3%)
    pallas_call x1, Pallas kernels, dense_body(): pl.pallas_call(functools.partial(kernel, subs, slabs), out_shape=pltpu.VM...  17 us
    add x1, other arithmetic, dense_body(): return (interface_k + gram[0], interface_m + gram[1])  0.63 us

profile of v9, /device:TPU:0, one launch (start us, length us, event | category | flops | bytes accessed | tf_op | source)
XLA Modules:
  0.0 18.3 jit_solution(1049940479551499769)
XLA Ops:
  0.6 0.0 copy-start
  0.6 0.0 copy-start.1
  0.7 17.0 %shard_map.104 = f32[2,2,32,128]{3,2,1,0:T(8,128)S(1)} custom-call(s32[8,8]{1,0:T(8,128)} %adjacency_hbm.1, s32[16]{0:T(128)} %piece_slot_hbm.1, s32[1,2,8]{2,1,0:T(2,128)} %tile_range_hbm.1, f32[1,64]{1,0:T(1,128)} %eigenvalues_hbm.1, bf16[1,64,64]{2,1,0:T(8,128)(2,1)} %modes.1, bf16[1,64,1024]{2,1,0:T(8,128)(2,1)} %coupling_k.1, ...), custom_call_target="tpu_custom_call" | custom-call | tf_op jit(solution)/shard_map/pallas_call | solution.py:296
  17.6 0.0 copy-done
  17.6 0.0 copy-done.1
  17.6 0.6 %bitcast_add_fusion = (f32[2,32,128]{2,1,0:T(8,128)}, f32[2,32,128]{2,1,0:T(8,128)}) fusion(f32[2,32,128]{2,1,0:T(8,128)S(1)} %copy-done, f32[2,2,32,128]{3,2,1,0:T(8,128)S(1)} %shard_map.104, f32[2,32,128]{2,1,0:T(8,128)S(1)} %copy-done.1), kind=kLoop, calls=%fused_computation | loop fusion | flops 16384 | bytes 196608 | tf_op jit(solution)/shard_map/add | solution.py:335
Async XLA Ops:
  0.6 17.0 %copy-start = (f32[2,32,128]{2,1,0:T(8,128)S(1)}, f32[2,32,128]{2,1,0:T(8,128)}, u32[]{:S(2)}) copy-start(f32[2,32,128]{2,1,0:T(8,128)} %param.17) | copy-start | bytes 98308
  0.6 17.0 %copy-start.1 = (f32[2,32,128]{2,1,0:T(8,128)S(1)}, f32[2,32,128]{2,1,0:T(8,128)}, u32[]{:S(2)}) copy-start(f32[2,32,128]{2,1,0:T(8,128)} %param.16) | copy-start | bytes 98308

commit v10 on v9

--- a/solution.py
+++ b/solution.py
@@ -31,6 +31,7 @@
     piece_slot,
     tile_range,
     eigenvalues,
+    adjacency_rows,
     my_modes,
     tile_k,
     tile_m,
@@ -74,7 +75,8 @@
         for n, (whole, held) in enumerate(((eigenvalues_hbm, eigenvalues),))
     ]
     late.append(pltpu.make_async_copy(modes.at[0], my_modes, small_sem.at[4]))
-    for load in routing + late[1:] + loads:
+    late.append(pltpu.make_async_copy(adjacency_hbm, adjacency_rows, small_sem.at[5]))
+    for load in routing + late[1:2] + loads:
         load.start()
 
     barrier = pltpu.get_barrier_semaphore()
@@ -92,6 +94,7 @@
         pl.semaphore_signal(barrier, inc=1, device_id=(sub, home), device_id_type=MESH)
 
     late[0].start()
+    late[2].start()
     late[1].wait()
     half = rows // 2
     all_modes[slab] = jnp.concatenate([my_modes[:half], my_modes[half:]], axis=1)
@@ -176,16 +179,14 @@
             columns[step, 0, slab] = tile_k[place] * live[step, 0]
             columns[step, 1, slab] = tile_m[place] * live[step, 0]
 
+    late[2].wait()
     takes = []
-    for other in range(subs):
-        theirs = [piece_slot[adjacency[other, a]] for a in range(adj)]
-        takes.append([
-            functools.reduce(
-                lambda x, y: x | y,
-                [(slot == sub * owned + q).astype(jnp.int32) for slot in theirs],
-            )
-            for q in range(owned)
-        ])
+    for q in range(owned):
+        piece = jnp.int32(0)
+        for p in range(piece_slot.shape[0]):
+            piece = jnp.where(piece_slot[p] == sub * owned + q, jnp.int32(p), piece)
+        hits = (adjacency_rows[...] == piece).astype(jnp.float32)
+        takes.append(jnp.max(hits, axis=1, keepdims=True))
     late[0].wait()
     eig = jnp.broadcast_to(eigenvalues[...], (width, modes.shape[2])).T
     root = lax.rsqrt(eig)
@@ -265,10 +266,14 @@
                 theirs = arrived.at[other, kind]
                 pltpu.make_async_copy(theirs, theirs, blocks_recv.at[other, kind]).wait()
 
+        taken = [
+            jnp.broadcast_to(takes[q][other : other + 1], (quarter, width)) > 0
+            for q in range(owned)
+        ]
         for kind in range(2):
             term = arrived[other, kind].astype(jnp.float32)
             for q in range(owned):
-                total[kind][q] = total[kind][q] + jnp.where(takes[other][q] > 0, term, 0.0)
+                total[kind][q] = total[kind][q] + jnp.where(taken[q], term, 0.0)
     for q in range(owned):
         gram[0, q] = total[0][q]
         gram[1, q] = total[1][q]
@@ -303,6 +308,7 @@
             pltpu.SMEM(piece_slot.shape, piece_slot.dtype),
             pltpu.SMEM(tile_range.shape, tile_range.dtype),
             pltpu.VMEM(eigenvalues.shape, eigenvalues.dtype),
+            pltpu.VMEM(adjacency.shape, adjacency.dtype),
             pltpu.VMEM((rows, mode_count), jnp.bfloat16),
             pltpu.VMEM((adj, rows, width), jnp.bfloat16),
             pltpu.VMEM((adj, rows, width), jnp.bfloat16),
@@ -311,7 +317,7 @@
             pltpu.VMEM((slabs, rows // 2, 2 * mode_count), jnp.bfloat16),
             pltpu.VMEM((group, 2, slabs, quarter, width), jnp.bfloat16),
             pltpu.VMEM((subs, 2, quarter, width), jnp.bfloat16),
-            pltpu.SemaphoreType.DMA((5,)),
+            pltpu.SemaphoreType.DMA((6,)),
             pltpu.SemaphoreType.DMA((2, adj)),
             pltpu.SemaphoreType.DMA((slabs - 1,)),
             pltpu.SemaphoreType.DMA((slabs,)),

time: 18.5 us -> 18.5 us (level)
  no operation moved by 1% of the time
where the time goes in v10:
time: 18.5 us; the launch traced here: 18.3 us
  Pallas kernels  17 us (92%)
  between operations  0.67 us (4%)
  other arithmetic  0.63 us (3%)
    pallas_call x1, Pallas kernels, dense_body(): pl.pallas_call(functools.partial(kernel, subs, slabs), out_shape=pltpu.VM...  17 us
    add x1, other arithmetic, dense_body(): return (interface_k + gram[0], interface_m + gram[1])  0.63 us

profile of v10, /device:TPU:0, one launch (start us, length us, event | category | flops | bytes accessed | tf_op | source)
XLA Modules:
  0.0 18.3 jit_solution(9476503661467680344)
XLA Ops:
  0.6 0.0 copy-start
  0.6 0.0 copy-start.1
  0.7 17.0 %shard_map.104 = f32[2,2,32,128]{3,2,1,0:T(8,128)S(1)} custom-call(s32[8,8]{1,0:T(8,128)} %adjacency_hbm.1, s32[16]{0:T(128)} %piece_slot_hbm.1, s32[1,2,8]{2,1,0:T(2,128)} %tile_range_hbm.1, f32[1,64]{1,0:T(1,128)} %eigenvalues_hbm.1, bf16[1,64,64]{2,1,0:T(8,128)(2,1)} %modes.1, bf16[1,64,1024]{2,1,0:T(8,128)(2,1)} %coupling_k.1, ...), custom_call_target="tpu_custom_call" | custom-call | tf_op jit(solution)/shard_map/pallas_call | solution.py:301
  17.6 0.0 copy-done
  17.6 0.0 copy-done.1
  17.6 0.6 %bitcast_add_fusion = (f32[2,32,128]{2,1,0:T(8,128)}, f32[2,32,128]{2,1,0:T(8,128)}) fusion(f32[2,32,128]{2,1,0:T(8,128)S(1)} %copy-done, f32[2,2,32,128]{3,2,1,0:T(8,128)S(1)} %shard_map.104, f32[2,32,128]{2,1,0:T(8,128)S(1)} %copy-done.1), kind=kLoop, calls=%fused_computation | loop fusion | flops 16384 | bytes 196608 | tf_op jit(solution)/shard_map/add | solution.py:341
Async XLA Ops:
  0.6 17.0 %copy-start = (f32[2,32,128]{2,1,0:T(8,128)S(1)}, f32[2,32,128]{2,1,0:T(8,128)}, u32[]{:S(2)}) copy-start(f32[2,32,128]{2,1,0:T(8,128)} %param.17) | copy-start | bytes 98308
  0.6 17.0 %copy-start.1 = (f32[2,32,128]{2,1,0:T(8,128)S(1)}, f32[2,32,128]{2,1,0:T(8,128)}, u32[]{:S(2)}) copy-start(f32[2,32,128]{2,1,0:T(8,128)} %param.16) | copy-start | bytes 98308

commit v11 on v9

--- a/solution.py
+++ b/solution.py
@@ -99,6 +99,8 @@
         load.wait()
     slots = [piece_slot[adjacency[sub, a]] for a in range(adj)]
 
+    far_first = sorted(range(1, slabs), key=lambda turn: abs(slabs - 2 * turn))
+
     def owner_of(part, step):
         return part + slabs * lax.rem(step + sub // slabs + 1, group)
 
@@ -130,7 +132,7 @@
     sends = []
 
     def send_columns(step, kind):
-        for turn in range(1, slabs):
+        for turn in far_first:
             part = lax.rem(slab + turn, slabs)
             copy = pltpu.make_async_remote_copy(
                 src_ref=outgoing.at[step, kind, turn - 1],
@@ -153,7 +155,7 @@
     def _():
         pl.semaphore_wait(barrier, slabs - 1 + group * slabs - 1)
 
-    for turn in range(1, slabs):
+    for turn in far_first:
         part = lax.rem(slab + turn, slabs)
         copy = pltpu.make_async_remote_copy(
             src_ref=all_modes.at[slab],
@@ -225,7 +227,7 @@
                     jnp.concatenate([second, third]), jnp.concatenate([second, -third])
                 )
             blocks[step, kind] = gram_part.astype(jnp.bfloat16).reshape(slabs, quarter, width)
-            for turn in range(1, slabs + 1):
+            for turn in far_first + [slabs]:
                 part = lax.rem(slab + turn, slabs)
                 copy = pltpu.make_async_remote_copy(
                     src_ref=blocks.at[step, kind, part],

time: 18.5 us -> 18.3 us (0.989)
  Pallas kernels: 17 us -> 16.8 us
where the time goes in v11:
time: 18.3 us; the launch traced here: 18.2 us
  Pallas kernels  16.8 us (92%)
  between operations  0.67 us (4%)
  other arithmetic  0.63 us (3%)
    pallas_call x1, Pallas kernels, dense_body(): pl.pallas_call(functools.partial(kernel, subs, slabs), out_shape=pltpu.VM...  16.8 us
    add x1, other arithmetic, dense_body(): return (interface_k + gram[0], interface_m + gram[1])  0.63 us

profile of v11, /device:TPU:0, one launch (start us, length us, event | category | flops | bytes accessed | tf_op | source)
XLA Modules:
  0.0 18.2 jit_solution(14204066751220944796)
XLA Ops:
  0.6 0.0 copy-start
  0.6 0.0 copy-start.1
  0.7 16.8 %shard_map.104 = f32[2,2,32,128]{3,2,1,0:T(8,128)S(1)} custom-call(s32[8,8]{1,0:T(8,128)} %adjacency_hbm.1, s32[16]{0:T(128)} %piece_slot_hbm.1, s32[1,2,8]{2,1,0:T(2,128)} %tile_range_hbm.1, f32[1,64]{1,0:T(1,128)} %eigenvalues_hbm.1, bf16[1,64,64]{2,1,0:T(8,128)(2,1)} %modes.1, bf16[1,64,1024]{2,1,0:T(8,128)(2,1)} %coupling_k.1, ...), custom_call_target="tpu_custom_call" | custom-call | tf_op jit(solution)/shard_map/pallas_call | solution.py:298
  17.5 0.0 copy-done
  17.5 0.0 copy-done.1
  17.5 0.6 %bitcast_add_fusion = (f32[2,32,128]{2,1,0:T(8,128)}, f32[2,32,128]{2,1,0:T(8,128)}) fusion(f32[2,32,128]{2,1,0:T(8,128)S(1)} %copy-done, f32[2,2,32,128]{3,2,1,0:T(8,128)S(1)} %shard_map.104, f32[2,32,128]{2,1,0:T(8,128)S(1)} %copy-done.1), kind=kLoop, calls=%fused_computation | loop fusion | flops 16384 | bytes 196608 | tf_op jit(solution)/shard_map/add | solution.py:337
Async XLA Ops:
  0.6 16.9 %copy-start = (f32[2,32,128]{2,1,0:T(8,128)S(1)}, f32[2,32,128]{2,1,0:T(8,128)}, u32[]{:S(2)}) copy-start(f32[2,32,128]{2,1,0:T(8,128)} %param.17) | copy-start | bytes 98308
  0.6 16.9 %copy-start.1 = (f32[2,32,128]{2,1,0:T(8,128)S(1)}, f32[2,32,128]{2,1,0:T(8,128)}, u32[]{:S(2)}) copy-start(f32[2,32,128]{2,1,0:T(8,128)} %param.16) | copy-start | bytes 98308
